TPU v7x, 32 devices: a whole 2x2x4 slice. The times are simulated.
32 devices in a mesh: fsdp: 4 (over x, core), ctx: 2 (over y), tp: 4 (over z).
Axes of the slice: x: 2, y: 2, z: 4, core: 2. Of those that a mesh axis runs over, the one named last changes fastest.
Arguments:
- tokens: bfloat16 [4, 2048, 2048], P('fsdp', ('ctx', 'tp')), may hold values from -48 to 48
- segments: int32 [4, 2048], P('fsdp', 'ctx'), may hold values from 0 to 7, as said below
- positions: int32 [4, 2048], P('fsdp', 'ctx'), may hold values from 0 to 2047, as said below
- norm_gain: bfloat16 [2048], P(('fsdp', 'ctx')), may hold values from 0.25 to 1.75
- norm_bias: bfloat16 [2048], P(('fsdp', 'ctx')), may hold values from -3 to 3
- projection_weight: bfloat16 [2048, 3, 2048], P(('fsdp', 'ctx'), None, 'tp'), may hold values from -0.125 to 0.125
- projection_bias: bfloat16 [3, 2048], P(None, 'tp'), may hold values from -3 to 3
- dense_weight: bfloat16 [2048, 2048], P(('fsdp', 'ctx'), 'tp'), may hold values from -0.75 to 0.75
- dense_bias: bfloat16 [2048], P(('fsdp', 'ctx')), may hold values from -3 to 3
- up_weight: bfloat16 [2048, 8192], P(('fsdp', 'ctx'), 'tp'), may hold values from -0.125 to 0.125
- up_bias: bfloat16 [8192], P('tp'), may hold values from -3 to 3
- down_weight: bfloat16 [2048, 8192], P(('fsdp', 'ctx'), 'tp'), may hold values from -0.0625 to 0.0625
- down_bias: bfloat16 [2048], P(('fsdp', 'ctx')), may hold values from -3 to 3
- cotangent: bfloat16 [4, 2048, 2048], P('fsdp', ('ctx', 'tp')), may hold values from -6 to 6
Outputs:
- layer_output: bfloat16 [4, 2048, 2048], P('fsdp', ('ctx', 'tp'))
- input_grad: float32 [4, 2048, 2048], P('fsdp', ('ctx', 'tp'))
- norm_gain_grad: float32 [2048], P(('fsdp', 'ctx'))
- norm_bias_grad: float32 [2048], P(('fsdp', 'ctx'))
- projection_weight_grad: float32 [2048, 3, 2048], P(('fsdp', 'ctx'), None, 'tp')
- projection_bias_grad: float32 [3, 2048], P(None, 'tp')
- dense_weight_grad: float32 [2048, 2048], P(('fsdp', 'ctx'), 'tp')
- dense_bias_grad: float32 [2048], P(('fsdp', 'ctx'))
- up_weight_grad: float32 [2048, 8192], P(('fsdp', 'ctx'), 'tp')
- up_bias_grad: float32 [8192], P('tp')
- down_weight_grad: float32 [2048, 8192], P(('fsdp', 'ctx'), 'tp')
- down_bias_grad: float32 [2048], P(('fsdp', 'ctx'))
Inputs may be any that keep to these rules, and one draw needn't show every extreme that they name: `segments`: each sequence holds exactly 8 documents, numbered from 0 in order of place; the tokens at places 2048 // 4 to 1536 of every sequence lie in one document. A token's position counts from its document's first token, except in the first document of a sequence, whose positions run up to 2047 at its last token.
All inputs are finite; a program needn't handle non-finite values.
Results may differ from a plain program's by a relative error of at most 0.011.
Values may be sent and summed in bfloat16 or wider, within the bound.
A program may use at most 192 MiB of HBM per device.

v0:
```python
import functools
import math

import jax
import jax.numpy as jnp
from jax import lax
from jax.experimental import pallas as pl
from jax.experimental.pallas import tpu as pltpu
from jax.sharding import PartitionSpec as P

HD = 64
ROT = 32
TILE = 256

epsilon = 1e-05
big_negative = -1000000000.0
root_two_over_pi = 0.7978845608028654
contract_rows = (((0,), (0,)), ((), ()))
contract_cols = (((1,), (1,)), ((), ()))
row_by_col = (((0,), (1,)), ((), ()))
MESH = pl.DeviceIdType.MESH
ANY = pl.BlockSpec(memory_space=pl.ANY)
VMEM = pl.BlockSpec(memory_space=pltpu.VMEM)
SMEM = pl.BlockSpec(memory_space=pltpu.SMEM)
DMA = pltpu.SemaphoreType.DMA
f32 = jnp.float32
bf16 = jnp.bfloat16


def layer_norm(values, gain_full, shift_full):
    center = jnp.mean(values, axis=-1, keepdims=True)
    centered = values - center
    spread = jnp.mean(centered * centered, axis=-1, keepdims=True)
    return centered * lax.rsqrt(spread + epsilon) * gain_full + shift_full


def gelu_and_slope(values):
    turned = jnp.tanh(root_two_over_pi * (values + 0.044715 * values * values * values))
    slope = 0.5 * (1.0 + turned) + 0.5 * values * (1.0 - turned * turned) * root_two_over_pi * (
        1.0 + 3.0 * 0.044715 * values * values
    )
    return 0.5 * values * (1.0 + turned), slope


class Place:
    def __init__(self, sizes):
        self.chips = sizes["fsdp"] // 2
        self.halves = sizes["ctx"]
        self.depth = sizes["tp"]
        lane = lax.axis_index("fsdp")
        self.chip = lane // 2
        self.core = lane % 2
        self.half = lax.axis_index("ctx")
        self.layer = lax.axis_index("tp")

    def device(self, chip=None, core=None, half=None, layer=None):
        chip = self.chip if chip is None else chip
        core = self.core if core is None else core
        half = self.half if half is None else half
        layer = self.layer if layer is None else layer
        return (chip * 2 + core, half, layer)

    def block(self, chip=None, core=None, half=None):
        chip = self.chip if chip is None else chip
        core = self.core if core is None else core
        half = self.half if half is None else half
        return (chip * 2 + core) * self.halves + half

    def ahead(self, k):
        return (self.chip + k) % self.chips

    def behind(self, k):
        return (self.chip + self.chips - k) % self.chips

    def pair(self):
        return self.device(core=1 - self.core)

    def across(self):
        return self.device(half=1 - self.half)

    def group(self):
        found = []
        for k in range(self.chips):
            for core in range(2):
                for half in range(2):
                    if k or core or half:
                        found.append(
                            (self.ahead(k), (self.core + core) % 2, (self.half + half) % 2)
                        )
        return found


def greet(devices):
    barrier = pltpu.get_barrier_semaphore()
    for device in devices:
        pl.semaphore_signal(barrier, inc=1, device_id=device, device_id_type=MESH)
    pl.semaphore_wait(barrier, len(devices))


def send(source, target, send_sem, recv_sem, device):
    return pltpu.make_async_remote_copy(
        src_ref=source,
        dst_ref=target,
        send_sem=send_sem,
        recv_sem=recv_sem,
        device_id=device,
        device_id_type=MESH,
    )


def plane(place):
    found = [place.device(chip=place.ahead(k)) for k in range(1, place.chips)]
    return found + [place.across(), place.pair()]


def reduce(sizes, paired, turned, rights, splits, small, collective_id, name):
    chips, halves = sizes["fsdp"] // 2, sizes["ctx"]
    groups = chips * halves
    paired_count, made_count = len(paired), len(rights)
    weight_count = paired_count + made_count
    block_rows = paired[0].shape[1]
    widths = [v.shape[2] for v in paired] + [v.shape[0] for _, v in rights]
    side = block_rows // 2

    def kernel(*refs):
        refs = list(refs)

        def take(count):
            taken = refs[:count]
            del refs[:count]
            return taken

        paired_in = take(paired_count)
        turned_in = take(2 * paired_count)
        lefts = [take(len(left)) for left, _ in rights]
        factors = take(made_count)
        (small_ref,) = take(1)
        weight_out = take(weight_count)
        (small_out,) = take(1)
        made = take(made_count)
        own, turn_a, turn_b, near = (take(weight_count) for _ in range(4))
        pair = [None] * paired_count + take(made_count)
        load_sem, core_send, core_recv = take(3)
        turn_send, turn_recv, near_send, near_recv = take(4)
        small_pair, small_near, small_far, small_send, small_recv = take(5)
        place = Place(sizes)
        greet(plane(place))
        pending = []

        def launch(copy, condition=None):
            if condition is None:
                copy.start()
            else:
                pl.when(condition)(copy.start)
            pending.append((copy, condition))

        other = 1 - place.core
        for a in range(paired_count):
            needed = [place.ahead(k) * halves + place.half for k in range(1, chips)]
            needed += [place.chip * halves + half for half in range(halves)]
            for number in needed:
                pltpu.make_async_copy(
                    paired_in[a].at[number], own[a].at[number], load_sem.at[a, number]
                ).start()
            for way, target in enumerate((turn_a[a], turn_b[a])):
                for k in range(1, chips):
                    pltpu.make_async_copy(
                        turned_in[2 * a + way].at[k - 1],
                        target.at[k - 1],
                        turn_recv.at[a, way, k],
                    ).start()

        def make(a):
            at = a - paired_count
            rows = made[at].shape[0] // len(lefts[at])
            for number, left in enumerate(lefts[at]):
                span = pl.ds(number * rows, rows)
                multiply("tt", [(left, factors[at])], [made[at].at[span]])
            for number in range(groups):
                chip, half = number // halves, number % halves
                theirs = place.block(chip, other, half)
                mine = place.block(chip, place.core, half)
                launch(
                    send(
                        made[at].at[pl.ds(pl.multiple_of(theirs * block_rows, 16), block_rows)],
                        pair[a].at[number],
                        core_send.at[a, number],
                        core_recv.at[a, number],
                        place.pair(),
                    )
                )
                pltpu.make_async_copy(
                    made[at].at[pl.ds(pl.multiple_of(mine * block_rows, 16), block_rows)],
                    own[a].at[number],
                    load_sem.at[a, number],
                ).start()

        def pair_sum(a, number):
            mine = own[a].at[number]
            pltpu.make_async_copy(mine, mine, load_sem.at[a, number]).wait()
            if a < paired_count:
                return
            theirs = pair[a].at[number]
            send(
                theirs, theirs, core_send.at[a, number], core_recv.at[a, number], place.pair()
            ).wait_recv()

            @pl.loop(0, block_rows, step=16)
            def _(r):
                at = pl.ds(pl.multiple_of(r, 16), 16)
                mine[at, :] = (mine[at, :].astype(f32) + theirs[at, :].astype(f32)).astype(bf16)

        def diagonal(a):
            for k in range(1, chips):
                number = place.ahead(k) * halves + 1 - place.half
                pair_sum(a, number)
                launch(
                    send(
                        own[a].at[number, pl.ds(0, side)],
                        turn_a[a].at[k - 1],
                        turn_send.at[a, 0, k],
                        turn_recv.at[a, 0, k],
                        place.across(),
                    )
                )
                launch(
                    send(
                        own[a].at[number, pl.ds(side, side)],
                        turn_b[a].at[k - 1],
                        turn_send.at[a, 1, k],
                        turn_recv.at[a, 1, k],
                        place.device(chip=place.ahead(k)),
                    )
                )

        def direct_pairs(a):
            for k in range(1, chips):
                pair_sum(a, place.ahead(k) * halves + place.half)
            pair_sum(a, place.chip * halves + 1 - place.half)

        def add_turn(a, number, first, refs_at):
            @pl.loop(0, side, step=16)
            def _(r):
                at = pl.ds(pl.multiple_of(first + r, 16), 16)
                total = own[a][number, at, :].astype(f32)
                for ref, k in refs_at:
                    total += ref[k, pl.ds(pl.multiple_of(r, 16), 16), :].astype(f32)
                own[a][number, at, :] = total.astype(bf16)

        def turn_wait(a, way, k):
            piece = (turn_a, turn_b)[way][a].at[k - 1]
            if a < paired_count:
                pltpu.make_async_copy(piece, piece, turn_recv.at[a, way, k]).wait()
            else:
                send(
                    piece, piece, turn_send.at[a, way, k], turn_recv.at[a, way, k], place.across()
                ).wait_recv()

        def direct(a):
            for k in range(1, chips):
                number = place.ahead(k) * halves + place.half
                turn_wait(a, 0, k)
                add_turn(a, number, 0, [(turn_a[a], k - 1)])
                launch(
                    send(
                        own[a].at[number],
                        near[a].at[k],
                        near_send.at[a, k],
                        near_recv.at[a, k],
                        place.device(chip=place.ahead(k)),
                    )
                )
            for k in range(1, chips):
                turn_wait(a, 1, k)
            number = place.chip * halves + 1 - place.half
            add_turn(a, number, side, [(turn_b[a], k - 1) for k in range(1, chips)])
            launch(
                send(
                    own[a].at[number],
                    near[a].at[0],
                    near_send.at[a, 0],
                    near_recv.at[a, 0],
                    place.across(),
                )
            )

        def finish(a):
            for k in range(chips):
                piece = near[a].at[k]
                send(
                    piece, piece, near_send.at[a, k], near_recv.at[a, k], place.across()
                ).wait_recv()
            number = place.chip * halves + place.half

            @pl.loop(0, block_rows, step=16)
            def _(r):
                at = pl.ds(pl.multiple_of(r, 16), 16)
                total = own[a][number, at, :].astype(f32) + near[a][0, at, :].astype(f32)
                for k in range(1, chips):
                    total += near[a][k, at, :].astype(f32)
                if splits[a] == 1:
                    weight_out[a][at, :] = total
                else:
                    wide = widths[a] // splits[a]
                    for kind in range(splits[a]):
                        weight_out[a][kind, at, :] = total[:, kind * wide : (kind + 1) * wide]

        def swap_small(source, target, at, device):
            copy = send(source, target, small_send.at[at], small_recv.at[at], device)
            launch(copy)
            return copy

        swap_small(small_ref, small_pair, 0, place.pair())
        for a in range(paired_count):
            direct_pairs(a)
            direct(a)
        for a in range(paired_count, weight_count):
            make(a)
        send(small_pair, small_pair, small_send.at[0], small_recv.at[0], place.pair()).wait_recv()
        small_near[0] = small_ref[...] + small_pair[...]
        for k in range(1, chips):
            swap_small(small_near.at[0], small_near.at[k], k, place.device(chip=place.ahead(k)))
        for a in range(paired_count, weight_count):
            diagonal(a)
            direct_pairs(a)
        total = small_near[0]
        for k in range(1, chips):
            piece = small_near.at[k]
            send(piece, piece, small_send.at[k], small_recv.at[k], place.pair()).wait_recv()
            total += small_near[k]
        small_far[0] = total
        swap_small(small_far.at[0], small_far.at[1], chips, place.across())
        for a in range(weight_count):
            pair_sum(a, place.chip * halves + place.half)
        for a in range(paired_count, weight_count):
            direct(a)
        for a in range(weight_count):
            finish(a)
        piece = small_far.at[1]
        send(piece, piece, small_send.at[chips], small_recv.at[chips], place.pair()).wait_recv()
        small_out[...] = small_far[0] + small_far[1]
        for copy, condition in pending:
            if condition is None:
                copy.wait_send()
            else:
                pl.when(condition)(copy.wait_send)

    shapes = [
        jax.ShapeDtypeStruct((block_rows, w) if n == 1 else (n, block_rows, w // n), f32)
        for w, n in zip(widths, splits)
    ]
    shapes.append(jax.ShapeDtypeStruct(small.shape, f32))
    made_shapes = [
        jax.ShapeDtypeStruct((2 * groups * block_rows, w), bf16) for w in widths[paired_count:]
    ]
    scratch = [pltpu.VMEM((groups, block_rows, w), bf16) for w in widths]
    scratch += [pltpu.VMEM((chips - 1, side, w), bf16) for w in widths] * 2
    scratch += [pltpu.VMEM((chips, block_rows, w), bf16) for w in widths]
    scratch += [pltpu.VMEM((groups, block_rows, w), bf16) for w in widths[paired_count:]]
    scratch += [
        DMA((weight_count, groups)),
        DMA((weight_count, groups)),
        DMA((weight_count, groups)),
        DMA((weight_count, 2, chips)),
        DMA((weight_count, 2, chips)),
        DMA((weight_count, chips)),
        DMA((weight_count, chips)),
        pltpu.VMEM(small.shape, f32),
        pltpu.VMEM((chips,) + small.shape, f32),
        pltpu.VMEM((2,) + small.shape, f32),
        DMA((chips + 1,)),
        DMA((chips + 1,)),
    ]
    lefts = [v for left, _ in rights for v in left]
    factors = [v for _, v in rights]
    return pl.pallas_call(
        kernel,
        out_shape=tuple(shapes + made_shapes),
        in_specs=[ANY] * (3 * paired_count + len(lefts) + made_count) + [VMEM],
        out_specs=(VMEM,) * len(shapes) + (ANY,) * made_count,
        scratch_shapes=scratch,
        compiler_params=pltpu.CompilerParams(
            collective_id=collective_id, has_side_effects=True, vmem_limit_bytes=60 << 20
        ),
        cost_estimate=pl.CostEstimate(flops=0, bytes_accessed=400_000_000, transcendentals=0),
        name=name,
    )(*paired, *turned, *lefts, *factors, small)[: weight_count + 1]


def multiply(kind, parts, outs, finish=None, extra=(), tile=512):
    dims = (((0 if kind[0] == "t" else 1,), (1 if kind[1] == "t" else 0,)), ((), ()))
    left, right = parts[0]
    rows = left.shape[1] if kind[0] == "t" else left.shape[0]
    width = right.shape[0] if kind[1] == "t" else right.shape[1]
    tile = min(tile, width)
    specs = []
    for left, right in parts:
        specs.append(pl.BlockSpec(left.shape, lambda n: (0, 0)))
        if kind[1] == "t":
            specs.append(pl.BlockSpec((tile, right.shape[1]), lambda n: (n, 0)))
        else:
            specs.append(pl.BlockSpec((right.shape[0], tile), lambda n: (0, n)))
    specs += [pl.BlockSpec((v.shape[0], tile), lambda n: (0, n)) for v in extra]

    def step(*refs):
        found = None
        for number in range(len(parts)):
            product = lax.dot_general(
                refs[2 * number][...],
                refs[2 * number + 1][...],
                dims,
                preferred_element_type=f32,
            )
            found = product if found is None else found + product
        rest = refs[2 * len(parts) :]
        results = (found,)
        if finish is not None:
            results = finish(found, *(v[...] for v in rest[: len(extra)]))
        for ref, value in zip(rest[len(extra) :], results):
            ref[...] = value.astype(ref.dtype)

    factors = [v for pair in parts for v in pair]
    pltpu.emit_pipeline(
        step,
        grid=(width // tile,),
        in_specs=specs,
        out_specs=[pl.BlockSpec((rows, tile), lambda n: (0, n))] * len(outs),
    )(*factors, *extra, *outs)


def half_rows(ref, half, count):
    return ref.at[pl.ds(pl.multiple_of(half * count, count), count)]


def front(
    sizes, tokens, cotangent, vectors, numbers, weights, projection_bias, up_bias, cosine, sine
):
    chips, halves, depth = sizes["fsdp"] // 2, sizes["ctx"], sizes["tp"]
    groups = sizes["fsdp"] * halves
    own_len, model = tokens.shape
    length = own_len * depth
    projection, up, dense, down = weights
    weight_count = len(weights)
    kinds, local = projection.shape[0], projection.shape[2]
    count = local // 2
    hidden = up.shape[1]
    shard = vectors.shape[1]
    half_rot = ROT // 2
    early_width = model // 2

    def kernel(*refs):
        refs = list(refs)

        def take(number):
            taken = refs[:number]
            del refs[:number]
            return taken

        tokens_ref, cotangent_ref, vector_ref, number_ref = take(4)
        weight_in = take(weight_count)
        bias_ref, up_bias_ref, cosine_ref, sine_ref = take(4)
        vectors_out, numbers_out, normed, cotangent_rows = take(4)
        weight_out = take(weight_count)
        both, activation, slope, triple = take(4)
        landed, normed_own, stage = take(3)
        vector_send, vector_recv, single, line_send, line_recv = take(5)
        keep, near_send, near_recv, turn_send, turn_recv, core_send, core_recv = take(7)
        place = Place(sizes)
        peers = place.group()
        up_there, down_there = place.layer < depth - 1, place.layer > 0
        above = place.device(layer=jnp.minimum(place.layer + 1, depth - 1))
        below = place.device(layer=jnp.maximum(place.layer - 1, 0))
        barrier = pltpu.get_barrier_semaphore()
        for chip, core, half in peers:
            pl.semaphore_signal(
                barrier,
                inc=1,
                device_id=place.device(chip=chip, core=core, half=half),
                device_id_type=MESH,
            )
        for there, device in ((up_there, above), (down_there, below)):

            @pl.when(there)
            def _(device=device):
                pl.semaphore_signal(barrier, inc=1, device_id=device, device_id_type=MESH)

        pl.semaphore_wait(
            barrier,
            len(peers) + up_there.astype(jnp.int32) + down_there.astype(jnp.int32),
        )
        pending = []

        def launch(copy, condition=None):
            if condition is None:
                copy.start()
            else:
                pl.when(condition)(copy.start)
            pending.append((copy, condition))

        def part(a, block, first=0, rows=None):
            rows = weight_in[a].shape[-2] if rows is None else rows
            start = pl.multiple_of(block * weight_in[a].shape[-2] + first, 16)
            span = pl.ds(start, rows)
            return weight_out[a].at[:, span] if a == 0 else weight_out[a].at[span]

        def arrive(piece, recv_sem):
            send(piece, piece, recv_sem, recv_sem, place.pair()).wait_recv()

        mine = place.block()
        vector_keep = pltpu.make_async_copy(vector_ref, landed.at[mine], single.at[0])
        vector_keep.start()
        for at, (chip, core, half) in enumerate(peers):
            launch(
                send(
                    vector_ref,
                    landed.at[mine],
                    vector_send.at[at],
                    vector_recv.at[at],
                    place.device(chip=chip, core=core, half=half),
                )
            )
        launch(send(number_ref, numbers_out, single.at[1], single.at[2], place.across()))

        def near_start(a):
            own = part(a, place.block())
            for k in range(1, chips):
                launch(
                    send(
                        weight_in[a],
                        own,
                        near_send.at[a, k],
                        near_recv.at[a, k],
                        place.device(chip=place.ahead(k)),
                    )
                )
            launch(
                send(weight_in[a], own, near_send.at[a, 0], near_recv.at[a, 0], place.across())
            )
            launch(send(weight_in[a], own, core_send.at[a, 0], core_recv.at[a, 0], place.pair()))
            pltpu.make_async_copy(weight_in[a], own, keep.at[a]).start()

        def near_step(a):
            side = weight_in[a].shape[-2] // 4
            rest = weight_in[a].shape[-2] - side
            for k in range(1, chips):
                block = place.block(chip=place.behind(k))
                piece = part(a, block)
                arrive(piece, near_recv.at[a, k])
                top = part(a, block, 0, side)
                launch(
                    send(top, top, turn_send.at[a, 0, k], turn_recv.at[a, 0, k], place.across())
                )
                launch(send(piece, piece, core_send.at[a, k], core_recv.at[a, k], place.pair()))
            block = place.block(half=1 - place.half)
            piece = part(a, block)
            arrive(piece, near_recv.at[a, 0])
            low = part(a, block, side, rest)
            for k in range(1, chips):
                launch(
                    send(
                        low,
                        low,
                        turn_send.at[a, 1, k],
                        turn_recv.at[a, 1, k],
                        place.device(chip=place.ahead(k)),
                    )
                )
            launch(
                send(piece, piece, core_send.at[a, chips], core_recv.at[a, chips], place.pair())
            )

        def turn_step(a):
            side = weight_in[a].shape[-2] // 4
            rest = weight_in[a].shape[-2] - side
            for k in range(1, chips):
                block = place.block(chip=place.behind(k), half=1 - place.half)
                arrive(part(a, block, 0, side), turn_recv.at[a, 0, k])
                arrive(part(a, block, side, rest), turn_recv.at[a, 1, k])
                piece = part(a, block)
                launch(
                    send(
                        piece,
                        piece,
                        core_send.at[a, chips + k],
                        core_recv.at[a, chips + k],
                        place.pair(),
                    )
                )

        def core_step(a):
            other = 1 - place.core
            blocks = [place.block(core=other)]
            blocks += [place.block(place.behind(k), other) for k in range(1, chips)]
            blocks += [place.block(None, other, 1 - place.half)]
            blocks += [
                place.block(place.behind(k), other, 1 - place.half) for k in range(1, chips)
            ]
            for at, block in enumerate(blocks):
                arrive(part(a, block), core_recv.at[a, at])
            pltpu.make_async_copy(weight_in[a], part(a, place.block()), keep.at[a]).wait()

        near_start(0)

        vector_keep.wait()
        for at in range(len(peers)):
            place_in = at + 1
            source = place.block(
                place.behind(place_in // 4),
                (place.core + place_in // 2 % 2) % 2,
                (place.half + place_in % 2) % 2,
            )
            arrive(landed.at[source], vector_recv.at[at])
        for number in range(groups):
            vectors_out[:, number * shard : (number + 1) * shard] = landed[number]

        @pl.loop(0, own_len, step=32)
        def _(r):
            at = pl.ds(pl.multiple_of(r, 32), 32)
            values = tokens_ref[at, :].astype(f32)
            normed_own[at, :] = layer_norm(
                values, vectors_out[0:1, :], vectors_out[1:2, :]
            ).astype(bf16)

        early = cotangent_ref.at[:, pl.ds(0, early_width)]
        line_own, line_full = (normed_own, early), (normed, cotangent_rows)

        def line(number, source):
            return line_full[number].at[pl.ds(pl.multiple_of(source * own_len, 16), own_len)]

        def line_keep(number):
            return pltpu.make_async_copy(
                line_own[number], line(number, place.layer), single.at[(3, 8)[number]]
            )

        def line_start(number):
            for way, (there, device) in enumerate(((up_there, above), (down_there, below))):
                launch(
                    send(
                        line_own[number],
                        line(number, place.layer),
                        line_send.at[number, way, 0],
                        line_recv.at[number, way, 0],
                        device,
                    ),
                    there,
                )
            line_keep(number).start()

        def line_step(number, k):
            for way, (onward, device) in enumerate(((up_there, above), (down_there, below))):
                source = place.layer - k if way == 0 else place.layer + k
                there = (source >= 0) & (source < depth)
                piece = line(number, jnp.clip(source, 0, depth - 1))
                arrived = send(
                    piece,
                    piece,
                    line_send.at[number, way, k - 1],
                    line_recv.at[number, way, k - 1],
                    device,
                )
                pl.when(there)(arrived.wait_recv)
                if k < depth - 1:
                    launch(
                        send(
                            piece,
                            piece,
                            line_send.at[number, way, k],
                            line_recv.at[number, way, k],
                            device,
                        ),
                        there & onward,
                    )

        line_start(0)
        near_start(1)
        near_step(0)
        line_step(0, 1)
        near_start(3)
        near_start(2)
        turn_step(0)
        near_step(1)
        for k in range(2, depth):
            line_step(0, k)
        line_start(1)
        line_keep(0).wait()
        core_step(0)
        near_step(3)

        def project(weight, rows, cosine_here, sine_here, out):
            for kind in range(kinds):
                found = lax.dot_general(
                    weight[kind], rows[...], row_by_col, preferred_element_type=f32
                )
                found = found + bias_ref[kind * local : (kind + 1) * local, :]
                if kind == 2:
                    out[kind] = found.astype(bf16)
                    continue
                for head in range(local // HD):
                    first = head * HD
                    leading = found[first : first + half_rot]
                    trailing = found[first + half_rot : first + ROT]
                    turned = (
                        leading * cosine_here[...] - trailing * sine_here[...],
                        trailing * cosine_here[...] + leading * sine_here[...],
                        found[first + ROT : first + HD],
                    )
                    out[kind, first : first + HD] = jnp.concatenate(turned, axis=0).astype(bf16)

        tile = min(512, length)
        pltpu.emit_pipeline(
            project,
            grid=(length // tile,),
            in_specs=[
                pl.BlockSpec(weight_out[0].shape, lambda n: (0, 0, 0)),
                pl.BlockSpec((tile, model), lambda n: (n, 0)),
                pl.BlockSpec((half_rot, tile), lambda n: (0, n)),
                pl.BlockSpec((half_rot, tile), lambda n: (0, n)),
            ],
            out_specs=[pl.BlockSpec((kinds, local, tile), lambda n: (0, 0, n))],
        )(weight_out[0], normed, cosine_ref, sine_ref, triple)

        def heads(half):
            return triple.at[:, pl.ds(pl.multiple_of(half * count, count), count)]

        here, there = place.half, 1 - place.half
        launch(send(heads(there), both.at[here], single.at[4], single.at[5], place.across()))
        load = pltpu.make_async_copy(heads(here), stage, single.at[6])
        load.start()
        load.wait()
        stage_keep = pltpu.make_async_copy(stage, both.at[here], single.at[7])
        stage_keep.start()
        near_step(2)
        line_step(1, 1)
        turn_step(1)
        core_step(1)
        wide = hidden // 2
        for number in range(2):
            span = pl.ds(number * wide, wide)
            multiply(
                "nn",
                [(normed, weight_out[1].at[:, span])],
                [activation.at[:, span], slope.at[:, span]],
                lambda found, bias: gelu_and_slope(found + bias),
                [up_bias_ref.at[:, span]],
            )
            if number == 0 and depth > 2:
                line_step(1, 2)
        turn_step(3)
        core_step(3)
        turn_step(2)
        core_step(2)
        for k in range(3, depth):
            line_step(1, k)
        line_keep(1).wait()
        stage_keep.wait()
        arrive(both.at[there], single.at[5])
        arrive(numbers_out, single.at[2])
        for copy, condition in pending:
            if condition is None:
                copy.wait_send()
            else:
                pl.when(condition)(copy.wait_send)

    out_shape = [
        jax.ShapeDtypeStruct((vectors.shape[0], groups * shard), f32),
        jax.ShapeDtypeStruct(numbers.shape, numbers.dtype),
        jax.ShapeDtypeStruct((length, model), bf16),
        jax.ShapeDtypeStruct((length, early_width), bf16),
    ]
    out_shape += [
        jax.ShapeDtypeStruct(v.shape[:-2] + (groups * v.shape[-2], v.shape[-1]), v.dtype)
        for v in weights
    ]
    out_shape += [
        jax.ShapeDtypeStruct((2, kinds, count, length), bf16),
        jax.ShapeDtypeStruct((length, hidden), bf16),
        jax.ShapeDtypeStruct((length, hidden), bf16),
        jax.ShapeDtypeStruct((kinds, local, length), bf16),
    ]
    results = pl.pallas_call(
        kernel,
        out_shape=tuple(out_shape),
        in_specs=[VMEM] * (4 + weight_count) + [VMEM, ANY, ANY, ANY],
        out_specs=(VMEM, VMEM) + (ANY,) * (len(out_shape) - 2),
        scratch_shapes=[
            pltpu.VMEM((groups,) + vectors.shape, f32),
            pltpu.VMEM((own_len, model), bf16),
            pltpu.VMEM((kinds, count, length), bf16),
            DMA((groups - 1,)),
            DMA((groups - 1,)),
            DMA((9,)),
            DMA((2, 2, depth - 1)),
            DMA((2, 2, depth - 1)),
            DMA((weight_count,)),
            DMA((weight_count, chips)),
            DMA((weight_count, chips)),
            DMA((weight_count, 2, chips)),
            DMA((weight_count, 2, chips)),
            DMA((weight_count, 2 * chips)),
            DMA((weight_count, 2 * chips)),
        ],
        compiler_params=pltpu.CompilerParams(
            collective_id=0, has_side_effects=True, vmem_limit_bytes=60 << 20
        ),
        cost_estimate=pl.CostEstimate(flops=0, bytes_accessed=480_000_000, transcendentals=0),
        name="front",
    )(tokens, cotangent, vectors, numbers, *weights, projection_bias, up_bias, cosine, sine)
    return results[:-1]


def exchange_attended(sizes, attended, activation, down_full, dense_full):
    width, total = attended.shape
    length = total // 2
    rows, model = activation.shape[0], down_full.shape[0]

    def kernel(attended_ref, activation_ref, down_ref, dense_ref, *rest):
        full, block_out, feed, stage, sems = rest
        place = Place(sizes)
        greet([place.across()])
        here, there = place.half, 1 - place.half

        def tokens(half):
            return attended_ref.at[:, pl.ds(pl.multiple_of(half * length, length), length)]

        away = send(
            tokens(there), half_rows(full, here, width), sems.at[0], sems.at[1], place.across()
        )
        load = pltpu.make_async_copy(tokens(here), stage, sems.at[2])
        keep = pltpu.make_async_copy(stage, half_rows(full, here, width), sems.at[3])
        away.start()
        load.start()
        load.wait()
        keep.start()
        multiply("nt", [(activation_ref, down_ref)], [feed])
        keep.wait()
        away.wait_send()
        came = half_rows(full, there, width)
        send(came, came, sems.at[0], sems.at[1], place.across()).wait_recv()
        multiply(
            "tt",
            [(full, dense_ref)],
            [block_out],
            lambda found, before: (found + before,),
            [feed],
        )

    return pl.pallas_call(
        kernel,
        out_shape=(
            jax.ShapeDtypeStruct((2 * width, length), bf16),
            jax.ShapeDtypeStruct((rows, model), bf16),
            jax.ShapeDtypeStruct((rows, model), f32),
        ),
        in_specs=[ANY] * 4,
        out_specs=(ANY,) * 3,
        scratch_shapes=[pltpu.VMEM((width, length), bf16), DMA((4,))],
        compiler_params=pltpu.CompilerParams(
            collective_id=4, has_side_effects=True, vmem_limit_bytes=60 << 20
        ),
        cost_estimate=pl.CostEstimate(flops=0, bytes_accessed=90_000_000, transcendentals=0),
        name="exchange_attended",
    )(attended, activation, down_full, dense_full)[:2]


def exchange_gradient(sizes, cotangents, dense_full, down_full, slope):
    rows, hidden = slope.shape
    local = dense_full.shape[1]
    width = local // 2
    count = len(cotangents)

    def kernel(*refs):
        cotangent_refs, (dense_ref, down_ref, slope_ref) = refs[:count], refs[count : count + 3]
        both, grad_hidden, made, stage, sems = refs[count + 3 :]
        place = Place(sizes)
        greet([place.across()])
        here, there = place.half, 1 - place.half

        def parts(weight_ref):
            found, first = [], 0
            for ref in cotangent_refs:
                found.append((ref, weight_ref.at[pl.ds(first, ref.shape[1])]))
                first += ref.shape[1]
            return found

        multiply("tt", [(b, a) for a, b in parts(dense_ref)], [made])
        away = send(
            half_rows(made, there, width), both.at[here], sems.at[0], sems.at[1], place.across()
        )
        load = pltpu.make_async_copy(half_rows(made, here, width), stage, sems.at[2])
        keep = pltpu.make_async_copy(stage, both.at[here], sems.at[3])
        away.start()
        load.start()
        load.wait()
        keep.start()
        multiply(
            "nn",
            parts(down_ref),
            [grad_hidden],
            lambda found, slope: (found * slope.astype(f32),),
            [slope_ref],
        )
        keep.wait()
        away.wait_send()
        came = both.at[there]
        send(came, came, sems.at[0], sems.at[1], place.across()).wait_recv()

    return pl.pallas_call(
        kernel,
        out_shape=(
            jax.ShapeDtypeStruct((2, width, rows), bf16),
            jax.ShapeDtypeStruct((rows, hidden), bf16),
            jax.ShapeDtypeStruct((local, rows), bf16),
        ),
        in_specs=[ANY] * (count + 3),
        out_specs=(ANY,) * 3,
        scratch_shapes=[pltpu.VMEM((width, rows), bf16), DMA((4,))],
        compiler_params=pltpu.CompilerParams(
            collective_id=5, has_side_effects=True, vmem_limit_bytes=60 << 20
        ),
        cost_estimate=pl.CostEstimate(flops=0, bytes_accessed=85_000_000, transcendentals=0),
        name="exchange_gradient",
    )(*cotangents, dense_full, down_full, slope)[:2]


def exchange_back(
    sizes, back, normed, grad_hidden, cotangents, activation, up_full, projection
):
    kinds, width, total = back.shape
    length = total // 2
    chips, halves = sizes["fsdp"] // 2, sizes["ctx"]
    rows, model = normed.shape
    hidden = grad_hidden.shape[1]
    span = model // (2 * chips)
    shard = span // halves
    side = shard // 2

    count = len(cotangents)

    def kernel(back_ref, normed_ref, hidden_ref, *rest):
        cotangent_refs, rest = rest[:count], rest[count:]
        (activation_ref, up_ref, weight_ref), rest = rest[:3], rest[3:]
        full, sums, turns, block_in = rest[0], rest[1:3], rest[3:7], rest[7]
        made_in, came_in, feed = rest[8:10], rest[10:12], rest[12]
        stage, sems, core_send, core_recv, turn_send, turn_recv = rest[13:]
        place = Place(sizes)
        greet(plane(place))
        here, there = place.half, 1 - place.half
        other = 1 - place.core

        def tokens(half):
            return back_ref.at[:, :, pl.ds(pl.multiple_of(half * length, length), length)]

        def heads(half):
            return full.at[:, pl.ds(pl.multiple_of(half * width, width), width)]

        away = send(tokens(there), heads(here), sems.at[0], sems.at[1], place.across())
        load = pltpu.make_async_copy(tokens(here), stage, sems.at[2])
        keep = pltpu.make_async_copy(stage, heads(here), sems.at[3])
        away.start()
        load.start()
        load.wait()
        keep.start()

        def to_pair(number):
            made, came = made_in[number], came_in[number]
            copies = []
            for chip in range(chips):
                copies.append(
                    send(
                        made.at[pl.ds(pl.multiple_of((2 * chip + other) * span, 16), span)],
                        came.at[pl.ds(chip * span, span)],
                        core_send.at[number, chip],
                        core_recv.at[number, chip],
                        place.pair(),
                    )
                )
                copies[-1].start()
            return copies

        def add_pair(number, copies):
            made, came, out = made_in[number], came_in[number], sums[number]
            for copy in copies:
                copy.wait()

            def step(mine, theirs, out_ref):
                out_ref[...] = (mine[...].astype(f32) + theirs[...].astype(f32)).astype(bf16)

            wide = hidden // 2
            pltpu.emit_pipeline(
                step,
                grid=(chips, 2),
                in_specs=[
                    pl.BlockSpec((span, wide), lambda i, j: (2 * i + place.core, j)),
                    pl.BlockSpec((span, wide), lambda i, j: (i, j)),
                ],
                out_specs=[pl.BlockSpec((span, wide), lambda i, j: (i, j))],
            )(made, came, out)

        def turn(number):
            out = sums[number]
            copies = []
            for k in range(1, chips):
                block = (place.ahead(k) * halves + there) * shard
                for way, device in enumerate(
                    (place.across(), place.device(chip=place.ahead(k)))
                ):
                    copies.append(
                        send(
                            out.at[pl.ds(pl.multiple_of(block + way * side, 16), side)],
                            turns[2 * number + way].at[k - 1],
                            turn_send.at[number, way, k],
                            turn_recv.at[number, way, k],
                            device,
                        )
                    )
                    copies[-1].start()
            return copies

        multiply("tn", [(normed_ref, hidden_ref)], [made_in[0]])
        up_copies = to_pair(0)
        first = 0
        for ref in cotangent_refs:
            span_of = pl.ds(first, ref.shape[1])
            multiply("tn", [(ref, activation_ref)], [made_in[1].at[span_of]])
            first += ref.shape[1]
        down_copies = to_pair(1)
        add_pair(0, up_copies)
        turned = turn(0)
        multiply("nt", [(hidden_ref, up_ref)], [feed])
        add_pair(1, down_copies)
        turned += turn(1)
        keep.wait()
        away.wait_send()
        send(heads(there), heads(there), sems.at[0], sems.at[1], place.across()).wait_recv()
        flat = full.reshape(2 * kinds * width, length)

        def step(left_ref, right_ref, before_ref, out_ref):
            found = before_ref[...]
            for kind in range(kinds):
                rows_of = pl.ds(kind * 2 * width, 2 * width)
                found += lax.dot_general(
                    left_ref[rows_of, :],
                    right_ref[kind],
                    row_by_col,
                    preferred_element_type=f32,
                )
            out_ref[...] = found.astype(bf16)

        tile = min(512, model)
        pltpu.emit_pipeline(
            step,
            grid=(model // tile,),
            in_specs=[
                pl.BlockSpec(flat.shape, lambda n: (0, 0)),
                pl.BlockSpec((kinds, tile, 2 * width), lambda n: (0, n, 0)),
                pl.BlockSpec((rows, tile), lambda n: (0, n)),
            ],
            out_specs=[pl.BlockSpec((rows, tile), lambda n: (0, n))],
        )(flat, weight_ref, feed, block_in)
        for copy in turned:
            copy.wait()

    product = jax.ShapeDtypeStruct((model, hidden), bf16)
    part = jax.ShapeDtypeStruct((model // 2, hidden), bf16)
    results = pl.pallas_call(
        kernel,
        out_shape=(
            jax.ShapeDtypeStruct((kinds, 2 * width, length), bf16),
            part,
            part,
            *[jax.ShapeDtypeStruct((chips - 1, side, hidden), bf16)] * 4,
            jax.ShapeDtypeStruct((rows, model), bf16),
            product,
            product,
            part,
            part,
            jax.ShapeDtypeStruct((rows, model), f32),
        ),
        in_specs=[ANY] * (6 + count),
        out_specs=(ANY,) * 13,
        scratch_shapes=[
            pltpu.VMEM((kinds, width, length), bf16),
            DMA((4,)),
            DMA((2, chips)),
            DMA((2, chips)),
            DMA((2, 2, chips)),
            DMA((2, 2, chips)),
        ],
        compiler_params=pltpu.CompilerParams(
            collective_id=6, has_side_effects=True, vmem_limit_bytes=60 << 20
        ),
        cost_estimate=pl.CostEstimate(flops=0, bytes_accessed=220_000_000, transcendentals=0),
        name="exchange_back",
    )(back, normed, grad_hidden, *cotangents, activation, up_full, projection)
    return results[:8]


def small_reduce(sizes, blocks):
    count, depth = sizes["fsdp"] * sizes["ctx"], sizes["tp"]

    def kernel(blocks_ref, out_ref, landed, line, send_sem, recv_sem, line_send, line_recv):
        place = Place(sizes)
        peers = place.group()
        layers = [(place.layer + k) % depth for k in range(1, depth)]
        devices = [place.device(chip=a, core=b, half=c) for a, b, c in peers]
        greet(devices + [place.device(layer=k) for k in layers])
        copies = []
        for at, (chip, core, half) in enumerate(peers):
            copy = send(
                blocks_ref.at[place.block(chip, core, half)],
                landed.at[at],
                send_sem.at[at],
                recv_sem.at[at],
                devices[at],
            )
            copy.start()
            copies.append(copy)
        total = blocks_ref[place.block()]
        for at, copy in enumerate(copies):
            copy.wait()
            total += landed[at]
        line[0] = total
        copies = []
        for k, layer in enumerate(layers):
            copy = send(
                line.at[0],
                line.at[k + 1],
                line_send.at[k],
                line_recv.at[k],
                place.device(layer=layer),
            )
            copy.start()
            copies.append(copy)
        for k, copy in enumerate(copies):
            copy.wait()
            total += line[k + 1]
        out_ref[...] = total

    block = blocks.shape[1:]
    return pl.pallas_call(
        kernel,
        out_shape=jax.ShapeDtypeStruct(block, f32),
        in_specs=[VMEM],
        out_specs=VMEM,
        scratch_shapes=[
            pltpu.VMEM((count - 1,) + block, f32),
            pltpu.VMEM((depth,) + block, f32),
            DMA((count - 1,)),
            DMA((count - 1,)),
            DMA((depth - 1,)),
            DMA((depth - 1,)),
        ],
        compiler_params=pltpu.CompilerParams(collective_id=3, has_side_effects=True),
        name="small_reduce",
    )(blocks)


def tile_at(number):
    return pl.ds(pl.multiple_of(number * TILE, TILE), TILE)


def allowed(kb, j, start):
    places = kb * TILE + lax.broadcasted_iota(jnp.int32, (TILE, TILE), 0)
    own = j * TILE + lax.broadcasted_iota(jnp.int32, (TILE, TILE), 1)
    return (places >= start) & (places <= own)


def attend_kernel(
    low_ref,
    mid_ref,
    triple_ref,
    start_ref,
    attended_ref,
    log_ref,
    query_t,
    key_t,
    value_t,
    key_rows,
    scores,
):
    length = triple_ref.shape[3]
    heads = triple_ref.shape[2] // HD
    score_scale = 1.0 / math.sqrt(HD)
    for number, ref in enumerate((query_t, key_t, value_t)):
        for part in range(2):
            piece = triple_ref[part, number]
            ref[:, part * length : (part + 1) * length] = (
                piece * score_scale if number == 0 else piece
            )
    rows = [slice(h * HD, (h + 1) * HD) for h in range(heads)]
    for h in range(heads):
        key_rows[h] = key_t[rows[h], :].T

    @pl.loop(0, 2 * length // TILE)
    def _(j):
        here = tile_at(j)
        start = start_ref[:, here]
        low, mid = low_ref[j], mid_ref[j]
        queries = [query_t[row, here] for row in rows]

        def score_with(masked):
            def score(kb, highest):
                ok = allowed(kb, j, start) if masked else None
                raised = []
                for h in range(heads):
                    found = jnp.dot(
                        key_rows[h, tile_at(kb), :], queries[h], preferred_element_type=f32
                    )
                    if masked:
                        found = jnp.where(ok, found, big_negative)
                    scores[h, tile_at(kb), :] = found
                    raised.append(
                        jnp.maximum(highest[h], jnp.max(found, axis=0, keepdims=True))
                    )
                return tuple(raised)

            return score

        highest = tuple(jnp.full((1, TILE), big_negative, f32) for _ in range(heads))
        highest = lax.fori_loop(low, mid, score_with(True), highest)
        highest = lax.fori_loop(mid, j, score_with(False), highest)
        highest = score_with(True)(j, highest)

        def weigh(kb, carry):
            after = []
            for h in range(heads):
                total, mixed = carry[h]
                prob = jnp.exp(scores[h, tile_at(kb), :] - highest[h])
                total = total + jnp.sum(prob, axis=0, keepdims=True)
                mixed = mixed + jnp.dot(
                    value_t[rows[h], tile_at(kb)], prob.astype(bf16), preferred_element_type=f32
                )
                after.append((total, mixed))
            return tuple(after)

        empty = tuple(
            (jnp.zeros((1, TILE), f32), jnp.zeros((HD, TILE), f32)) for _ in range(heads)
        )
        result = lax.fori_loop(low, j + 1, weigh, empty)
        for h in range(heads):
            total, mixed = result[h]
            attended_ref[rows[h], here] = (mixed / total).astype(bf16)
            log_ref[h, :, here] = highest[h] + jnp.log(total)


def turned_back(values, cosine, sine):
    half_rot = ROT // 2
    leading = values[:half_rot]
    trailing = values[half_rot:ROT]
    return jnp.concatenate(
        [
            leading * cosine + trailing * sine,
            trailing * cosine - leading * sine,
            values[ROT:],
        ],
        axis=0,
    )


def attend_back_kernel(
    low_ref,
    mid_ref,
    triple_ref,
    grad_ref,
    attended_ref,
    log_ref,
    start_ref,
    cosine_ref,
    sine_ref,
    back_ref,
    query_t,
    key_t,
    grad_t,
    key_rows,
    value_rows,
    key_sum,
    value_sum,
):
    length = triple_ref.shape[3]
    heads = triple_ref.shape[2] // HD
    score_scale = 1.0 / math.sqrt(HD)
    rows = [slice(h * HD, (h + 1) * HD) for h in range(heads)]
    for part in range(2):
        span = slice(part * length, (part + 1) * length)
        query_t[:, span] = triple_ref[part, 0] * score_scale
        key_t[:, span] = triple_ref[part, 1]
        grad_t[:, span] = grad_ref[part]
        for h in range(heads):
            value_rows[h, span, :] = triple_ref[part, 2, rows[h]].T
    for h in range(heads):
        key_rows[h] = key_t[rows[h], :].T
    key_sum[...] = jnp.zeros_like(key_sum)
    value_sum[...] = jnp.zeros_like(value_sum)

    @pl.loop(0, 2 * length // TILE)
    def _(j):
        here = tile_at(j)
        start = start_ref[:, here]
        low, mid = low_ref[j], mid_ref[j]
        queries = [query_t[row, here] for row in rows]
        grads = [grad_t[row, here] for row in rows]
        query_rows = [value.T for value in queries]
        grad_rows = [value.T for value in grads]
        logs = [log_ref[h, :, here] for h in range(heads)]
        deltas = [
            jnp.sum(
                grads[h].astype(f32) * attended_ref[rows[h], here].astype(f32),
                axis=0,
                keepdims=True,
            )
            for h in range(heads)
        ]

        def pull_with(masked):
            def pull(kb, query_back):
                ok = allowed(kb, j, start) if masked else None
                after = []
                for h in range(heads):
                    score = jnp.dot(
                        key_rows[h, tile_at(kb), :], queries[h], preferred_element_type=f32
                    )
                    if masked:
                        score = jnp.where(ok, score, big_negative)
                    prob = jnp.exp(score - logs[h])
                    down = jnp.dot(
                        value_rows[h, tile_at(kb), :], grads[h], preferred_element_type=f32
                    )
                    score_back = (prob * (down - deltas[h])).astype(bf16)
                    value_sum[h, tile_at(kb), :] += jnp.dot(
                        prob.astype(bf16), grad_rows[h], preferred_element_type=f32
                    )
                    key_sum[h, tile_at(kb), :] += jnp.dot(
                        score_back, query_rows[h], preferred_element_type=f32
                    )
                    after.append(
                        query_back[h]
                        + jnp.dot(
                            key_t[rows[h], tile_at(kb)], score_back, preferred_element_type=f32
                        )
                    )
                return tuple(after)

            return pull

        query_back = tuple(jnp.zeros((HD, TILE), f32) for _ in range(heads))
        query_back = lax.fori_loop(low, mid, pull_with(True), query_back)
        query_back = lax.fori_loop(mid, j, pull_with(False), query_back)
        query_back = pull_with(True)(j, query_back)
        for h in range(heads):
            back_ref[0, rows[h], here] = turned_back(
                query_back[h] * score_scale, cosine_ref[:, here], sine_ref[:, here]
            ).astype(bf16)

    for h in range(heads):
        back_ref[1, rows[h], :] = turned_back(
            key_sum[h].T, cosine_ref[...], sine_ref[...]
        ).astype(bf16)
        back_ref[2, rows[h], :] = value_sum[h].T.astype(bf16)


def attend(low, mid, triple, start):
    width, length = triple.shape[2], triple.shape[3]
    total, heads = 2 * length, width // HD
    area = total * total // 3 * heads
    return pl.pallas_call(
        attend_kernel,
        out_shape=(
            jax.ShapeDtypeStruct((width, total), bf16),
            jax.ShapeDtypeStruct((heads, 1, total), f32),
        ),
        in_specs=[SMEM, SMEM, VMEM, VMEM],
        out_specs=(VMEM, VMEM),
        scratch_shapes=[pltpu.VMEM((width, total), bf16)] * 3
        + [pltpu.VMEM((heads, total, HD), bf16), pltpu.VMEM((heads, total, TILE), f32)],
        compiler_params=pltpu.CompilerParams(vmem_limit_bytes=48 << 20),
        cost_estimate=pl.CostEstimate(
            flops=50 * area * HD, bytes_accessed=8 * width * total, transcendentals=area
        ),
        name="attend",
    )(low, mid, triple, start)


def attend_back(low, mid, triple, grad, attended, log_sum, start, cosine, sine):
    width, length = triple.shape[2], triple.shape[3]
    total, heads = 2 * length, width // HD
    area = total * total // 3 * heads
    return pl.pallas_call(
        attend_back_kernel,
        out_shape=jax.ShapeDtypeStruct((3, width, total), bf16),
        in_specs=[SMEM, SMEM] + [VMEM] * 7,
        out_specs=VMEM,
        scratch_shapes=[pltpu.VMEM((width, total), bf16)] * 3
        + [pltpu.VMEM((heads, total, HD), bf16)] * 2
        + [pltpu.VMEM((heads, total, HD), f32)] * 2,
        compiler_params=pltpu.CompilerParams(vmem_limit_bytes=48 << 20),
        cost_estimate=pl.CostEstimate(
            flops=100 * area * HD, bytes_accessed=12 * width * total, transcendentals=area
        ),
        name="attend_back",
    )(low, mid, triple, grad, attended, log_sum, start, cosine, sine)


def rotate_rows(values, cosine, sine):
    half_rot = ROT // 2
    leading = values[:, :half_rot]
    trailing = values[:, half_rot:ROT]
    return jnp.concatenate(
        [
            leading * cosine - trailing * sine,
            trailing * cosine + leading * sine,
            values[:, ROT:],
        ],
        axis=1,
    )


def ordered(*values):
    return lax.optimization_barrier(values)


def body(
    sizes,
    tokens,
    segments,
    positions,
    norm_gain,
    norm_bias,
    projection_weight,
    projection_bias,
    dense_weight,
    dense_bias,
    up_weight,
    up_bias,
    down_weight,
    down_bias,
    cotangent,
):
    own_len, model_width = tokens.shape[1], tokens.shape[2]
    half_len = segments.shape[1]
    local_width = projection_weight.shape[2]
    hidden_width = up_weight.shape[1]
    shard_rows = norm_gain.shape[0]
    half = lax.axis_index("ctx")
    total_len = 2 * half_len

    vectors = jnp.concatenate([norm_gain, norm_bias, dense_bias, down_bias]).astype(f32)
    vectors = jnp.pad(vectors.reshape(4, shard_rows), ((0, 4), (0, 0)))
    numbers = jnp.pad(jnp.concatenate([segments, positions], axis=0), ((0, 6), (0, 0)))
    exponent = jnp.arange(ROT // 2, dtype=f32) * 2.0 / ROT
    inverse = 10000.0 ** (-exponent)

    def angles(places_of):
        phase_angle = inverse[:, None] * places_of.astype(f32)[None, :]
        return jnp.cos(phase_angle), jnp.sin(phase_angle)

    cosine_own, sine_own = angles(positions[0])
    (
        vectors_full,
        numbers_other,
        normed,
        cotangent_early,
        projection,
        up_full,
        dense_full,
        down_full,
        both,
        activation,
        slope,
    ) = front(
        sizes,
        tokens[0],
        cotangent[0],
        vectors,
        numbers,
        [projection_weight.transpose(1, 0, 2), up_weight, dense_weight, down_weight],
        projection_bias.astype(f32).reshape(3 * local_width, 1),
        up_bias.astype(f32)[None, :],
        cosine_own,
        sine_own,
    )
    gain_full, shift_full, bias_dense, bias_down = (vectors_full[row] for row in range(4))

    cotangent_late, normed = ordered(cotangent[0, :, cotangent_early.shape[1] :], normed)
    cotangent_late = lax.all_gather(cotangent_late, "tp", axis=0, tiled=True)
    cotangents = [cotangent_early, cotangent_late]

    def in_order(own, other, axis):
        return jnp.where(
            half == 0,
            jnp.concatenate([own, other], axis=axis),
            jnp.concatenate([other, own], axis=axis),
        )

    sequence = in_order(numbers, numbers_other, 1)
    segment_row, position_row = sequence[0], sequence[1]
    places = jnp.arange(total_len, dtype=jnp.int32)
    edges = jnp.concatenate([jnp.ones((1,), bool), segment_row[1:] != segment_row[:-1]])
    start = lax.cummax(jnp.where(edges, places, 0))
    tile_count = total_len // TILE
    low = start[::TILE] // TILE
    mid = jnp.minimum(
        jnp.maximum((start[TILE - 1 :: TILE] + TILE - 1) // TILE, low),
        jnp.arange(tile_count, dtype=jnp.int32),
    )
    cosine_full, sine_full = angles(position_row)
    attended_heads, log_sum = attend(low, mid, both, start[None, :])
    attended, block_out = exchange_attended(
        sizes, attended_heads, activation, down_full, dense_full
    )
    branch_own = lax.psum_scatter(block_out, "tp", scatter_dimension=0, tiled=True)
    cotangent_late, block_out = ordered(cotangent_late, block_out)
    cotangents = [cotangent_early, cotangent_late]
    grad_both, grad_hidden = exchange_gradient(sizes, cotangents, dense_full, down_full, slope)
    back_heads = attend_back(
        low,
        mid,
        both,
        grad_both,
        attended_heads,
        log_sum,
        start[None, :],
        cosine_full,
        sine_full,
    )
    grad_projected, up_sum, down_sum, *turned, block_in = exchange_back(
        sizes, back_heads, normed, grad_hidden, cotangents, activation, up_full, projection
    )
    grad_projected = grad_projected.reshape(3 * local_width, half_len)
    block_in, branch_own = ordered(block_in, branch_own)
    grad_normed_own = lax.psum_scatter(block_in, "tp", scatter_dimension=0, tiled=True).astype(f32)
    hidden_sum = jnp.sum(grad_hidden.astype(f32), axis=0)
    projected_sum = jnp.sum(grad_projected.astype(f32), axis=1)
    small = jnp.concatenate([projected_sum, hidden_sum]).reshape(-1, 128)
    groups = sizes["fsdp"] // 2 * sizes["ctx"]
    up_part, down_part, projection_part, dense_part, small_total = reduce(
        sizes,
        [v.reshape(groups, shard_rows, hidden_width) for v in (up_sum, down_sum)],
        turned,
        [([normed], grad_projected), (cotangents, attended)],
        [1, 1, 3, 1],
        small,
        2,
        "reduce_weights",
    )
    tokens_late, grad_normed_own = ordered(tokens[0], grad_normed_own)
    inputs = tokens_late.astype(f32)
    _, norm_pull = jax.vjp(layer_norm, inputs, gain_full, shift_full)
    layer_output = (inputs + branch_own.astype(f32) + (bias_dense + bias_down)).astype(bf16)
    cotangent_own = cotangent[0].astype(f32)
    grad_inputs, grad_gain, grad_shift = norm_pull(grad_normed_own)
    input_grad = grad_inputs + cotangent_own
    output_sum = jnp.sum(cotangent_own, axis=0)
    sums = jnp.stack([grad_gain, grad_shift, output_sum]).reshape(3, -1, shard_rows)
    sums = jnp.pad(sums.transpose(1, 0, 2), ((0, 0), (0, 5), (0, 0)))
    totals = small_reduce(sizes, sums)
    small_flat = small_total.reshape(-1)
    return (
        layer_output[None],
        input_grad[None],
        totals[0],
        totals[1],
        projection_part.transpose(1, 0, 2),
        small_flat[: 3 * local_width].reshape(3, local_width),
        dense_part,
        totals[2],
        up_part,
        small_flat[3 * local_width :],
        down_part,
        totals[2],
    )


def solution(mesh):
    placed = (
        P("fsdp", ("ctx", "tp"), None),
        P("fsdp", "ctx"),
        P("fsdp", "ctx"),
        P(("fsdp", "ctx")),
        P(("fsdp", "ctx")),
        P(("fsdp", "ctx"), None, "tp"),
        P(None, "tp"),
        P(("fsdp", "ctx"), "tp"),
        P(("fsdp", "ctx")),
        P(("fsdp", "ctx"), "tp"),
        P("tp"),
        P(("fsdp", "ctx"), "tp"),
        P(("fsdp", "ctx")),
        P("fsdp", ("ctx", "tp"), None),
    )
    return jax.shard_map(
        functools.partial(body, dict(mesh.shape)),
        mesh=mesh,
        in_specs=placed,
        out_specs=(
            P("fsdp", ("ctx", "tp"), None),
            P("fsdp", ("ctx", "tp"), None),
            P(("fsdp", "ctx")),
            P(("fsdp", "ctx")),
            P(("fsdp", "ctx"), None, "tp"),
            P(None, "tp"),
            P(("fsdp", "ctx"), "tp"),
            P(("fsdp", "ctx")),
            P(("fsdp", "ctx"), "tp"),
            P("tp"),
            P(("fsdp", "ctx"), "tp"),
            P(("fsdp", "ctx")),
        ),
        check_vma=False,
    )
```

profile of v0, /device:TPU:0, one launch (start us, length us, event | category | flops | bytes accessed | tf_op | source)
XLA Modules:
  0.0 494.0 jit_solution(15211602166236805811)
XLA Ops:
  10.7 1.3 broadcast_in_dim.37
  12.0 1.9 slice_bitcast_fusion
  13.9 1.2 copy.28
  15.7 1.0 multiply_sine_fusion.1
  16.6 139.7 %front.1 = (f32[8,2048]{1,0:T(8,128)}, s32[8,1024]{1,0:T(8,128)}, bf16[1024,2048]{1,0:T(8,128)(2,1)}, bf16[1024,1024]{1,0:T(8,128)(2,1)}, bf16[3,2048,512]{2,1,0...) custom-call(bf16[256,2048]{1,0:T(8,128)(2,1)} %bitcast.46, ...), custom_call_target="tpu_custom_call" | custom-call | bytes 480000000 | tf_op jit(solution)/shard_map/front/pallas_call | solution.py:780
  156.3 11.7 %reduce-scatter.3.cloned.1.call-start = ((), (), s32[]{:S(2)}) async-start(), calls=%async_computation.3 | async-start | bytes 5242880 | tf_op jit(solution)/shard_map/reduce_scatter | solution.py:1510
  168.0 0.8 add_select_fusion
  169.9 1.9 copy-done.3
  171.9 20.0 %attend.1 = (bf16[256,2048]{1,0:T(8,128)(2,1)S(1)}, f32[4,1,2048]{2,1,0:T(1,128)S(1)}) custom-call(s32[8]{0:T(128)S(1)} %get-tuple-element.92.low_ref, s32[8]{0:T(128)S(1)} %get-tuple-element.91.mid_ref, bf16[2,3,256,1024]{3,2,1,0:T(8,128)(2,1)S(1)} %copy-done.3, s32[1,2048]{1,0:T(1,128)S(1)} %bitcast.44), custom_call_target="tpu_custom_call" | custom-call | flops 17895692288 | bytes 4194304 | tf_op jit(solution)/shard_map/attend/pallas_call | solution.py:1365
  191.9 1.0 copy-done.1
  192.8 26.4 %exchange_attended.1 = (bf16[512,1024]{1,0:T(8,128)(2,1)}, bf16[1024,2048]{1,0:T(8,128)(2,1)}, f32[1024,2048]{1,0:T(8,128)}) custom-call(bf16[256,2048]{1,0:T(8,128)(2,1)} %copy-done.1, bf16[1024,2048]{1,0:T(8,128)(2,1)} %get-tuple-element.55.activation_ref.rest_2_, bf16[2048,2048]{1,0:T(8,128)(2,1)} %get-tuple-element.56.down_ref.refs_3_, ...), custom_call_target="tpu_custom_call" | custom-call | bytes 90000000 | tf_op jit(solution)/shard_map/exchange_attended/pallas_call | solution.py:847
  219.9 24.8 %exchange_gradient.1 = (bf16[2,256,1024]{2,1,0:T(8,128)(2,1)}, bf16[1024,2048]{1,0:T(8,128)(2,1)}, bf16[512,1024]{1,0:T(8,128)(2,1)}) custom-call(bf16[1024,1024]{1,0:T(8,128)(2,1)} %get-tuple-element.51.refs_0_.rest_0_.refs_7_, bf16[1024,1024]{1,0:T(8,128)(2,1)} %all-gather.2.cloned.1.call-done.refs_1_.rest_1_.refs_8_, ...), custom_call_target="tpu_custom_call" | custom-call | bytes 85000000 | tf_op jit(solution)/shard_map/exchange_gradient/pallas_call | solution.py:907
  244.7 1.2 copy-done.4
  245.9 37.9 %attend_back.1.back_ref = bf16[3,256,2048]{2,1,0:T(8,128)(2,1)S(1)} custom-call(s32[8]{0:T(128)S(1)} %get-tuple-element.92.low_ref, s32[8]{0:T(128)S(1)} %get-tuple-element.91.mid_ref, bf16[2,3,256,1024]{3,2,1,0:T(8,128)(2,1)} %get-tuple-element.50.triple_ref, bf16[2,256,1024]{2,1,0:T(8,128)(2,1)S(1)} %copy-done.4, bf16[256,2048]{1,0:T(8,128)(2,1)S(1)} %copy-done.2, ...), custom_call_target="tpu_custom_call" | custom-call | flops 35791384576 | bytes 6291456 | tf_op jit(solution)/shard_map/attend_back/pallas_call | solution.py:1387
  283.8 1.6 copy-done
  285.4 77.4 %exchange_back.1 = (bf16[3,512,1024]{2,1,0:T(8,128)(2,1)}, bf16[1024,2048]{1,0:T(8,128)(2,1)}, bf16[1024,2048]{1,0:T(8,128)(2,1)}, bf16[1,128,2048]{2,1,0:T(8,12...) custom-call(bf16[3,256,2048]{2,1,0:T(8,128)(2,1)} %copy-done, ...), custom_call_target="tpu_custom_call" | custom-call | bytes 220000000 | tf_op jit(solution)/shard_map/exchange_back/pallas_call | solution.py:1065
  362.9 1.1 fusion.14
  363.9 0.9 copy-done.6
  365.3 2.8 convert_reduce_fusion
  368.8 88.7 %reduce_weights.1 = (f32[256,2048]{1,0:T(8,128)}, f32[256,2048]{1,0:T(8,128)}, f32[3,256,512]{2,1,0:T(8,128)}, f32[256,512]{1,0:T(8,128)}, f32[28,128]{1,0:T(8,1...) custom-call(bf16[4,256,2048]{2,1,0:T(8,128)(2,1)} %bitcast.53, bf16[4,256,2048]{2,1,0:T(8,128)(2,1)} %bitcast.54, ...), custom_call_target="tpu_custom_call" | custom-call | bytes 400000000 | tf_op jit(solution)/shard_map/reduce_weights/pallas_call | solution.py:376
  457.5 0.8 slice.72
  458.9 1.3 slice_bitcast_fusion.1
  460.2 1.5 convert_element_type.44
  462.6 1.0 fusion.8
  464.1 3.1 convert_reduce_fusion.3
  467.9 11.3 %small_reduce.1 = f32[8,256]{1,0:T(8,128)} custom-call(f32[8,8,256]{2,1,0:T(8,128)} %pad.17.blocks_ref), custom_call_target="tpu_custom_call" | custom-call | tf_op jit(solution)/shard_map/small_reduce/pallas_call | solution.py:1140
  479.2 1.4 fusion.15
  481.2 1.1 copy.35
  482.3 0.8 copy.36
  483.4 1.3 copy.37
  484.7 1.0 copy-done.8
  485.8 1.3 copy.38
  (66 shorter events, 10.5 us)
Async XLA Ops:
  7.2 212.7 %all-gather.2.cloned.1.call-start = ((), (), s32[]{:S(2)}) async-start(), calls=%async_computation.2 | async-start | bytes 2621440 | tf_op jit(solution)/shard_map/all_gather | solution.py:1484
  16.6 151.4 %copy-start.13 = (s32[8,1024]{1,0:T(8,128)S(1)}, s32[8,1024]{1,0:T(8,128)}, u32[]{:S(2)}) copy-start(s32[8,1024]{1,0:T(8,128)} %pad.14.refs_3_) | copy-start | bytes 98308
  156.3 206.5 %reduce-scatter.3.cloned.1.call-start = ((), (), s32[]{:S(2)}) async-start(), calls=%async_computation.3 | async-start | bytes 5242880 | tf_op jit(solution)/shard_map/reduce_scatter | solution.py:1510
  169.9 1.9 copy-start.3
  191.9 1.0 copy-start.1
  219.3 241.0 %reduce-scatter.5.cloned.1.call-start = ((), (), s32[]{:S(2)}) async-start(), calls=%async_computation.4 | async-start | bytes 5242880 | tf_op jit(solution)/shard_map/reduce_scatter | solution.py:1530
  219.9 24.8 %copy-start.2 = (bf16[256,2048]{1,0:T(8,128)(2,1)S(1)}, bf16[256,2048]{1,0:T(8,128)(2,1)}, u32[]{:S(2)}) copy-start(bf16[256,2048]{1,0:T(8,128)(2,1)} %copy-done.1) | copy-start | bytes 3145732
  244.7 1.2 copy-start.4
  283.8 1.6 copy-start
  362.8 2.0 copy-start.6
  457.5 4.2 copy-start.5
  462.6 1.2 copy-start.7
  462.6 1.5 copy-start.11
  464.1 17.0 %copy-start.10 = (f32[3,256,512]{2,1,0:T(8,128)S(1)}, f32[3,256,512]{2,1,0:T(8,128)}, u32[]{:S(2)}) copy-start(f32[3,256,512]{2,1,0:T(8,128)} %get-tuple-element.81) | copy-start | bytes 4718596
  467.2 15.1 %copy-start.12 = (f32[256,512]{1,0:T(8,128)S(1)}, f32[256,512]{1,0:T(8,128)}, u32[]{:S(2)}) copy-start(f32[256,512]{1,0:T(8,128)} %get-tuple-element.149) | copy-start | bytes 1572868
  480.6 2.5 copy-start.14
  481.1 2.3 copy-start.9
  483.4 2.3 copy-start.8
Sparse Core Ops, SparseCore 0:
  156.5 46.2 all-gather.1
  219.4 76.8 reduce-scatter.2
  363.0 76.8 reduce-scatter.4
where the time goes:
time: 497 us; the launch traced here: 494 us
  Pallas kernels  426 us (86%)
  local copies, waits for them, and re-layouts  22.4 us (5%)
  other arithmetic  19.2 us (4%)
  between operations  14.4 us (3%)
  starting transfers between devices  11.7 us (2%)
    pallas_call x1, Pallas kernels, front(): pl.pallas_call(kernel, out_shape=tuple(out_shape), in_specs=[VMEM] * (4 +...  140 us
    pallas_call x1, Pallas kernels, reduce(): pl.pallas_call(kernel, out_shape=tuple(shapes + made_shapes), in_specs=[A...  88.7 us
    pallas_call x1, Pallas kernels, exchange_back(): pl.pallas_call(kernel, out_shape=(jax.ShapeDtypeStruct((kinds, 2 * width,...  77.4 us
    pallas_call x1, Pallas kernels, attend_back(): pl.pallas_call(attend_back_kernel, out_shape=jax.ShapeDtypeStruct((3, wid...  37.9 us
    pallas_call x1, Pallas kernels, exchange_attended(): pl.pallas_call(kernel, out_shape=(jax.ShapeDtypeStruct((2 * width, length...  26.4 us
    pallas_call x1, Pallas kernels, exchange_gradient(): pl.pallas_call(kernel, out_shape=(jax.ShapeDtypeStruct((2, width, rows),...  24.8 us
    pallas_call x1, Pallas kernels, attend(): pl.pallas_call(attend_kernel, out_shape=(jax.ShapeDtypeStruct((width, tot...  20 us
    unnamed x37, local copies, waits for them, and re-layouts  14.8 us
  transfers between devices with their start and end apart: 3, of which 0 were waited for; matrix products, arithmetic and copies ran while one was open for 2% of the time, Pallas kernels for 56%

commit v1 on v0

--- a/solution.py
+++ b/solution.py
@@ -72,6 +72,13 @@
     def behind(self, k):
         return (self.chip + self.chips - k) % self.chips
 
+    def neighbours(self):
+        last = self.depth - 1
+        return (
+            (self.layer < last, self.device(layer=jnp.minimum(self.layer + 1, last))),
+            (self.layer > 0, self.device(layer=jnp.maximum(self.layer - 1, 0))),
+        )
+
     def pair(self):
         return self.device(core=1 - self.core)
 
@@ -97,6 +104,21 @@
     pl.semaphore_wait(barrier, len(devices))
 
 
+def greet_line(place, devices):
+    barrier = pltpu.get_barrier_semaphore()
+    for device in devices:
+        pl.semaphore_signal(barrier, inc=1, device_id=device, device_id_type=MESH)
+    count = len(devices)
+    for there, device in place.neighbours():
+
+        @pl.when(there)
+        def _(device=device):
+            pl.semaphore_signal(barrier, inc=1, device_id=device, device_id_type=MESH)
+
+        count = count + there.astype(jnp.int32)
+    pl.semaphore_wait(barrier, count)
+
+
 def send(source, target, send_sem, recv_sem, device):
     return pltpu.make_async_remote_copy(
         src_ref=source,
@@ -108,19 +130,59 @@
     )
 
 
+class Line:
+    def __init__(self, place, own, full, send_sem, recv_sem, keep_sem):
+        self.place, self.own, self.full = place, own, full
+        self.send_sem, self.recv_sem = send_sem, recv_sem
+        self.rows = own.shape[0]
+        self.pending = []
+        self.keep = pltpu.make_async_copy(own, self.block(place.layer), keep_sem)
+
+    def block(self, source):
+        return self.full.at[pl.ds(pl.multiple_of(source * self.rows, 16), self.rows)]
+
+    def copy(self, piece, target, way, hop, device):
+        return send(piece, target, self.send_sem.at[way, hop], self.recv_sem.at[way, hop], device)
+
+    def launch(self, copy, condition):
+        pl.when(condition)(copy.start)
+        self.pending.append((copy, condition))
+
+    def start(self):
+        for way, (there, device) in enumerate(self.place.neighbours()):
+            target = self.block(self.place.layer)
+            self.launch(self.copy(self.own, target, way, 0, device), there)
+        self.keep.start()
+
+    def step(self, k):
+        last = self.place.depth - 1
+        for way, (onward, device) in enumerate(self.place.neighbours()):
+            source = self.place.layer - k if way == 0 else self.place.layer + k
+            there = (source >= 0) & (source <= last)
+            piece = self.block(jnp.clip(source, 0, last))
+            pl.when(there)(self.copy(piece, piece, way, k - 1, device).wait_recv)
+            if k < last:
+                self.launch(self.copy(piece, piece, way, k, device), there & onward)
+
+    def end(self):
+        for copy, condition in self.pending:
+            pl.when(condition)(copy.wait_send)
+
+
 def plane(place):
     found = [place.device(chip=place.ahead(k)) for k in range(1, place.chips)]
     return found + [place.across(), place.pair()]
 
 
-def reduce(sizes, paired, turned, rights, splits, small, collective_id, name):
+def reduce(sizes, paired, turned, rights, small, collective_id, name):
     chips, halves = sizes["fsdp"] // 2, sizes["ctx"]
     groups = chips * halves
     paired_count, made_count = len(paired), len(rights)
     weight_count = paired_count + made_count
-    block_rows = paired[0].shape[1]
-    widths = [v.shape[2] for v in paired] + [v.shape[0] for _, v in rights]
-    side = block_rows // 2
+    whole_count = weight_count - 1
+    block_rows = paired[0][0].shape[0] // (2 * groups)
+    widths = [v.shape[1] for v, _ in paired] + [v.shape[0] for _, v in rights]
+    sides = [turned[2 * a].shape[1] for a in range(paired_count)] + [block_rows // 2] * made_count
 
     def kernel(*refs):
         refs = list(refs)
@@ -130,16 +192,17 @@
             del refs[:count]
             return taken
 
-        paired_in = take(paired_count)
+        paired_in = [take(2) for _ in range(paired_count)]
         turned_in = take(2 * paired_count)
         lefts = [take(len(left)) for left, _ in rights]
         factors = take(made_count)
         (small_ref,) = take(1)
-        weight_out = take(weight_count)
+        weight_out = take(whole_count)
         (small_out,) = take(1)
-        made = take(made_count)
-        own, turn_a, turn_b, near = (take(weight_count) for _ in range(4))
-        pair = [None] * paired_count + take(made_count)
+        held_out, made = take(weight_count - whole_count), take(made_count)
+        own, turn_a, turn_b = (take(weight_count) for _ in range(3))
+        near = take(whole_count)
+        pair = take(weight_count)
         load_sem, core_send, core_recv = take(3)
         turn_send, turn_recv, near_send, near_recv = take(4)
         small_pair, small_near, small_far, small_send, small_recv = take(5)
@@ -155,12 +218,22 @@
             pending.append((copy, condition))
 
         other = 1 - place.core
+        needed = [place.ahead(k) * halves + place.half for k in range(1, chips)]
+        needed += [place.chip * halves + 1 - place.half, place.chip * halves + place.half]
         for a in range(paired_count):
-            needed = [place.ahead(k) * halves + place.half for k in range(1, chips)]
-            needed += [place.chip * halves + half for half in range(halves)]
-            for number in needed:
+            for at, number in enumerate(needed):
+                chip = place.ahead(at + 1) if at < chips - 1 else place.chip
+                half = 1 - place.half if at == chips - 1 else place.half
+                mine = place.block(chip, place.core, half)
                 pltpu.make_async_copy(
-                    paired_in[a].at[number], own[a].at[number], load_sem.at[a, number]
+                    paired_in[a][0].at[pl.ds(pl.multiple_of(mine * block_rows, 16), block_rows)],
+                    own[a].at[number],
+                    load_sem.at[a, number],
+                ).start()
+                pltpu.make_async_copy(
+                    paired_in[a][1].at[pl.ds(pl.multiple_of(number * block_rows, 16), block_rows)],
+                    pair[a].at[at],
+                    core_recv.at[a, number],
                 ).start()
             for way, target in enumerate((turn_a[a], turn_b[a])):
                 for k in range(1, chips):
@@ -172,10 +245,11 @@
 
         def make(a):
             at = a - paired_count
-            rows = made[at].shape[0] // len(lefts[at])
-            for number, left in enumerate(lefts[at]):
-                span = pl.ds(number * rows, rows)
+            first = 0
+            for left in lefts[at]:
+                span = pl.ds(first, left.shape[1])
                 multiply("tt", [(left, factors[at])], [made[at].at[span]])
+                first += left.shape[1]
             for number in range(groups):
                 chip, half = number // halves, number % halves
                 theirs = place.block(chip, other, half)
@@ -195,15 +269,17 @@
                     load_sem.at[a, number],
                 ).start()
 
-        def pair_sum(a, number):
+        def pair_sum(a, number, at_needed=None):
             mine = own[a].at[number]
             pltpu.make_async_copy(mine, mine, load_sem.at[a, number]).wait()
             if a < paired_count:
-                return
-            theirs = pair[a].at[number]
-            send(
-                theirs, theirs, core_send.at[a, number], core_recv.at[a, number], place.pair()
-            ).wait_recv()
+                theirs = pair[a].at[at_needed]
+                pltpu.make_async_copy(theirs, theirs, core_recv.at[a, number]).wait()
+            else:
+                theirs = pair[a].at[number]
+                send(
+                    theirs, theirs, core_send.at[a, number], core_recv.at[a, number], place.pair()
+                ).wait_recv()
 
             @pl.loop(0, block_rows, step=16)
             def _(r):
@@ -216,7 +292,7 @@
                 pair_sum(a, number)
                 launch(
                     send(
-                        own[a].at[number, pl.ds(0, side)],
+                        own[a].at[number, pl.ds(0, sides[a])],
                         turn_a[a].at[k - 1],
                         turn_send.at[a, 0, k],
                         turn_recv.at[a, 0, k],
@@ -225,7 +301,7 @@
                 )
                 launch(
                     send(
-                        own[a].at[number, pl.ds(side, side)],
+                        own[a].at[number, pl.ds(sides[a], block_rows - sides[a])],
                         turn_b[a].at[k - 1],
                         turn_send.at[a, 1, k],
                         turn_recv.at[a, 1, k],
@@ -235,11 +311,11 @@
 
         def direct_pairs(a):
             for k in range(1, chips):
-                pair_sum(a, place.ahead(k) * halves + place.half)
-            pair_sum(a, place.chip * halves + 1 - place.half)
-
-        def add_turn(a, number, first, refs_at):
-            @pl.loop(0, side, step=16)
+                pair_sum(a, place.ahead(k) * halves + place.half, k - 1)
+            pair_sum(a, place.chip * halves + 1 - place.half, chips - 1)
+
+        def add_turn(a, number, first, count, refs_at):
+            @pl.loop(0, count, step=16)
             def _(r):
                 at = pl.ds(pl.multiple_of(first + r, 16), 16)
                 total = own[a][number, at, :].astype(f32)
@@ -256,11 +332,19 @@
                     piece, piece, turn_send.at[a, way, k], turn_recv.at[a, way, k], place.across()
                 ).wait_recv()
 
+        def hand(a, at, number):
+            pltpu.make_async_copy(
+                own[a].at[number], held_out[a - whole_count].at[at], near_send.at[a, at]
+            ).start()
+
         def direct(a):
             for k in range(1, chips):
                 number = place.ahead(k) * halves + place.half
                 turn_wait(a, 0, k)
-                add_turn(a, number, 0, [(turn_a[a], k - 1)])
+                add_turn(a, number, 0, sides[a], [(turn_a[a], k - 1)])
+                if a >= whole_count:
+                    hand(a, k, number)
+                    continue
                 launch(
                     send(
                         own[a].at[number],
@@ -273,7 +357,16 @@
             for k in range(1, chips):
                 turn_wait(a, 1, k)
             number = place.chip * halves + 1 - place.half
-            add_turn(a, number, side, [(turn_b[a], k - 1) for k in range(1, chips)])
+            add_turn(
+                a,
+                number,
+                sides[a],
+                block_rows - sides[a],
+                [(turn_b[a], k - 1) for k in range(1, chips)],
+            )
+            if a >= whole_count:
+                hand(a, 0, number)
+                return
             launch(
                 send(
                     own[a].at[number],
@@ -290,20 +383,16 @@
                 send(
                     piece, piece, near_send.at[a, k], near_recv.at[a, k], place.across()
                 ).wait_recv()
+                pltpu.make_async_copy(piece, weight_out[a].at[k], load_sem.at[a, k]).start()
             number = place.chip * halves + place.half
-
-            @pl.loop(0, block_rows, step=16)
-            def _(r):
-                at = pl.ds(pl.multiple_of(r, 16), 16)
-                total = own[a][number, at, :].astype(f32) + near[a][0, at, :].astype(f32)
-                for k in range(1, chips):
-                    total += near[a][k, at, :].astype(f32)
-                if splits[a] == 1:
-                    weight_out[a][at, :] = total
-                else:
-                    wide = widths[a] // splits[a]
-                    for kind in range(splits[a]):
-                        weight_out[a][kind, at, :] = total[:, kind * wide : (kind + 1) * wide]
+            pltpu.make_async_copy(
+                own[a].at[number], weight_out[a].at[chips], load_sem.at[a, chips]
+            ).start()
+
+        def finish_end(a):
+            for k in range(chips + 1):
+                piece = weight_out[a].at[k]
+                pltpu.make_async_copy(piece, piece, load_sem.at[a, k]).wait()
 
         def swap_small(source, target, at, device):
             copy = send(source, target, small_send.at[at], small_recv.at[at], device)
@@ -331,11 +420,19 @@
         small_far[0] = total
         swap_small(small_far.at[0], small_far.at[1], chips, place.across())
         for a in range(weight_count):
-            pair_sum(a, place.chip * halves + place.half)
+            pair_sum(a, place.chip * halves + place.half, chips)
         for a in range(paired_count, weight_count):
             direct(a)
-        for a in range(weight_count):
+            if a >= whole_count:
+                hand(a, chips, place.chip * halves + place.half)
+        for a in range(whole_count):
             finish(a)
+        for a in range(whole_count):
+            finish_end(a)
+        for a in range(whole_count, weight_count):
+            for at in range(chips + 1):
+                piece = held_out[a - whole_count].at[at]
+                pltpu.make_async_copy(piece, piece, near_send.at[a, at]).wait()
         piece = small_far.at[1]
         send(piece, piece, small_send.at[chips], small_recv.at[chips], place.pair()).wait_recv()
         small_out[...] = small_far[0] + small_far[1]
@@ -346,25 +443,29 @@
                 pl.when(condition)(copy.wait_send)
 
     shapes = [
-        jax.ShapeDtypeStruct((block_rows, w) if n == 1 else (n, block_rows, w // n), f32)
-        for w, n in zip(widths, splits)
+        jax.ShapeDtypeStruct((chips + 1, block_rows, w), bf16) for w in widths[:whole_count]
     ]
     shapes.append(jax.ShapeDtypeStruct(small.shape, f32))
+    held_shapes = [
+        jax.ShapeDtypeStruct((chips + 1, block_rows, w), bf16) for w in widths[whole_count:]
+    ]
     made_shapes = [
         jax.ShapeDtypeStruct((2 * groups * block_rows, w), bf16) for w in widths[paired_count:]
     ]
     scratch = [pltpu.VMEM((groups, block_rows, w), bf16) for w in widths]
-    scratch += [pltpu.VMEM((chips - 1, side, w), bf16) for w in widths] * 2
-    scratch += [pltpu.VMEM((chips, block_rows, w), bf16) for w in widths]
+    scratch += [pltpu.VMEM((chips - 1, n, w), bf16) for w, n in zip(widths, sides)]
+    scratch += [pltpu.VMEM((chips - 1, block_rows - n, w), bf16) for w, n in zip(widths, sides)]
+    scratch += [pltpu.VMEM((chips, block_rows, w), bf16) for w in widths[:whole_count]]
+    scratch += [pltpu.VMEM((chips + 1, block_rows, w), bf16) for w in widths[:paired_count]]
     scratch += [pltpu.VMEM((groups, block_rows, w), bf16) for w in widths[paired_count:]]
     scratch += [
-        DMA((weight_count, groups)),
+        DMA((weight_count, groups + 1)),
         DMA((weight_count, groups)),
         DMA((weight_count, groups)),
         DMA((weight_count, 2, chips)),
         DMA((weight_count, 2, chips)),
-        DMA((weight_count, chips)),
-        DMA((weight_count, chips)),
+        DMA((weight_count, chips + 1)),
+        DMA((weight_count, chips + 1)),
         pltpu.VMEM(small.shape, f32),
         pltpu.VMEM((chips,) + small.shape, f32),
         pltpu.VMEM((2,) + small.shape, f32),
@@ -375,16 +476,16 @@
     factors = [v for _, v in rights]
     return pl.pallas_call(
         kernel,
-        out_shape=tuple(shapes + made_shapes),
-        in_specs=[ANY] * (3 * paired_count + len(lefts) + made_count) + [VMEM],
-        out_specs=(VMEM,) * len(shapes) + (ANY,) * made_count,
+        out_shape=tuple(shapes + held_shapes + made_shapes),
+        in_specs=[ANY] * (4 * paired_count + len(lefts) + made_count) + [VMEM],
+        out_specs=(ANY,) * whole_count + (VMEM,) + (ANY,) * (weight_count - whole_count + made_count),
         scratch_shapes=scratch,
         compiler_params=pltpu.CompilerParams(
             collective_id=collective_id, has_side_effects=True, vmem_limit_bytes=60 << 20
         ),
         cost_estimate=pl.CostEstimate(flops=0, bytes_accessed=400_000_000, transcendentals=0),
         name=name,
-    )(*paired, *turned, *lefts, *factors, small)[: weight_count + 1]
+    )(*[v for two in paired for v in two], *turned, *lefts, *factors, small)[: weight_count + 1]
 
 
 def multiply(kind, parts, outs, finish=None, extra=(), tile=512):
@@ -424,7 +525,7 @@
         step,
         grid=(width // tile,),
         in_specs=specs,
-        out_specs=[pl.BlockSpec((rows, tile), lambda n: (0, n))] * len(outs),
+        out_specs=[pl.BlockSpec((v.shape[0], tile), lambda n: (0, n)) for v in outs],
     )(*factors, *extra, *outs)
 
 
@@ -432,9 +533,7 @@
     return ref.at[pl.ds(pl.multiple_of(half * count, count), count)]
 
 
-def front(
-    sizes, tokens, cotangent, vectors, numbers, weights, projection_bias, up_bias, cosine, sine
-):
+def front(sizes, tokens, cotangent, vectors, numbers, weights, projection_bias, up_bias):
     chips, halves, depth = sizes["fsdp"] // 2, sizes["ctx"], sizes["tp"]
     groups = sizes["fsdp"] * halves
     own_len, model = tokens.shape
@@ -444,9 +543,9 @@
     kinds, local = projection.shape[0], projection.shape[2]
     count = local // 2
     hidden = up.shape[1]
-    shard = vectors.shape[1]
+    shard = vectors[0].shape[0]
     half_rot = ROT // 2
-    early_width = model // 2
+    early_width = model // 4 * 3
 
     def kernel(*refs):
         refs = list(refs)
@@ -456,46 +555,25 @@
             del refs[:number]
             return taken
 
-        tokens_ref, cotangent_ref, vector_ref, number_ref = take(4)
+        tokens_ref, cotangent_ref = take(2)
+        vector_in, number_in = take(len(vectors)), take(len(numbers))
         weight_in = take(weight_count)
-        bias_ref, up_bias_ref, cosine_ref, sine_ref = take(4)
-        vectors_out, numbers_out, normed, cotangent_rows = take(4)
+        bias_in, up_bias_in = take(2)
+        vectors_out, *numbers_out = take(1 + len(numbers))
+        normed, cotangent_rows, cotangent_late = take(3)
         weight_out = take(weight_count)
         both, activation, slope, triple = take(4)
-        landed, normed_own, stage = take(3)
-        vector_send, vector_recv, single, line_send, line_recv = take(5)
+        landed, normed_own, stage, vector_ref, bias_ref, up_bias_ref, cosine_ref, sine_ref = take(8)
+        vector_send, vector_recv, number_sems, single, line_send, line_recv = take(6)
         keep, near_send, near_recv, turn_send, turn_recv, core_send, core_recv = take(7)
         place = Place(sizes)
         peers = place.group()
-        up_there, down_there = place.layer < depth - 1, place.layer > 0
-        above = place.device(layer=jnp.minimum(place.layer + 1, depth - 1))
-        below = place.device(layer=jnp.maximum(place.layer - 1, 0))
-        barrier = pltpu.get_barrier_semaphore()
-        for chip, core, half in peers:
-            pl.semaphore_signal(
-                barrier,
-                inc=1,
-                device_id=place.device(chip=chip, core=core, half=half),
-                device_id_type=MESH,
-            )
-        for there, device in ((up_there, above), (down_there, below)):
-
-            @pl.when(there)
-            def _(device=device):
-                pl.semaphore_signal(barrier, inc=1, device_id=device, device_id_type=MESH)
-
-        pl.semaphore_wait(
-            barrier,
-            len(peers) + up_there.astype(jnp.int32) + down_there.astype(jnp.int32),
-        )
+        greet_line(place, [place.device(chip=a, core=b, half=c) for a, b, c in peers])
         pending = []
 
-        def launch(copy, condition=None):
-            if condition is None:
-                copy.start()
-            else:
-                pl.when(condition)(copy.start)
-            pending.append((copy, condition))
+        def launch(copy):
+            copy.start()
+            pending.append(copy)
 
         def part(a, block, first=0, rows=None):
             rows = weight_in[a].shape[-2] if rows is None else rows
@@ -507,6 +585,9 @@
             send(piece, piece, recv_sem, recv_sem, place.pair()).wait_recv()
 
         mine = place.block()
+        vector_ref[...] = jnp.zeros_like(vector_ref)
+        for row, ref in enumerate(vector_in):
+            vector_ref[row : row + 1, :] = ref[...].astype(f32).reshape(1, shard)
         vector_keep = pltpu.make_async_copy(vector_ref, landed.at[mine], single.at[0])
         vector_keep.start()
         for at, (chip, core, half) in enumerate(peers):
@@ -519,7 +600,16 @@
                     place.device(chip=chip, core=core, half=half),
                 )
             )
-        launch(send(number_ref, numbers_out, single.at[1], single.at[2], place.across()))
+        for number in range(len(numbers)):
+            launch(
+                send(
+                    number_in[number],
+                    numbers_out[number],
+                    number_sems.at[0, number],
+                    number_sems.at[1, number],
+                    place.across(),
+                )
+            )
 
         def near_start(a):
             own = part(a, place.block())
@@ -622,67 +712,38 @@
             ).astype(bf16)
 
         early = cotangent_ref.at[:, pl.ds(0, early_width)]
-        line_own, line_full = (normed_own, early), (normed, cotangent_rows)
-
-        def line(number, source):
-            return line_full[number].at[pl.ds(pl.multiple_of(source * own_len, 16), own_len)]
-
-        def line_keep(number):
-            return pltpu.make_async_copy(
-                line_own[number], line(number, place.layer), single.at[(3, 8)[number]]
-            )
-
-        def line_start(number):
-            for way, (there, device) in enumerate(((up_there, above), (down_there, below))):
-                launch(
-                    send(
-                        line_own[number],
-                        line(number, place.layer),
-                        line_send.at[number, way, 0],
-                        line_recv.at[number, way, 0],
-                        device,
-                    ),
-                    there,
-                )
-            line_keep(number).start()
-
-        def line_step(number, k):
-            for way, (onward, device) in enumerate(((up_there, above), (down_there, below))):
-                source = place.layer - k if way == 0 else place.layer + k
-                there = (source >= 0) & (source < depth)
-                piece = line(number, jnp.clip(source, 0, depth - 1))
-                arrived = send(
-                    piece,
-                    piece,
-                    line_send.at[number, way, k - 1],
-                    line_recv.at[number, way, k - 1],
-                    device,
-                )
-                pl.when(there)(arrived.wait_recv)
-                if k < depth - 1:
-                    launch(
-                        send(
-                            piece,
-                            piece,
-                            line_send.at[number, way, k],
-                            line_recv.at[number, way, k],
-                            device,
-                        ),
-                        there & onward,
-                    )
-
-        line_start(0)
+        lines = (
+            Line(place, normed_own, normed, line_send.at[0], line_recv.at[0], single.at[3]),
+            Line(place, early, cotangent_rows, line_send.at[1], line_recv.at[1], single.at[8]),
+        )
+
+        lines[0].start()
         near_start(1)
+        late_keep = pltpu.make_async_copy(
+            cotangent_ref.at[:, pl.ds(early_width, model - early_width)],
+            cotangent_late,
+            single.at[1],
+        )
+        late_keep.start()
+        bias_ref[...] = bias_in[...].astype(f32).T
+        up_bias_ref[...] = up_bias_in[...].astype(f32).reshape(1, hidden)
+        turns = lax.broadcasted_iota(jnp.int32, (half_rot, 1), 0)
+        inverse = jnp.zeros((half_rot, 1), f32)
+        for row in range(half_rot):
+            inverse = jnp.where(turns == row, 10000.0 ** (-2.0 * row / ROT), inverse)
+        phase = inverse * number_in[1][...].astype(f32)
+        cosine_ref[...] = jnp.cos(phase)
+        sine_ref[...] = jnp.sin(phase)
         near_step(0)
-        line_step(0, 1)
+        lines[0].step(1)
         near_start(3)
         near_start(2)
         turn_step(0)
         near_step(1)
         for k in range(2, depth):
-            line_step(0, k)
-        line_start(1)
-        line_keep(0).wait()
+            lines[0].step(k)
+        lines[1].start()
+        lines[0].keep.wait()
         core_step(0)
         near_step(3)
 
@@ -691,7 +752,7 @@
                 found = lax.dot_general(
                     weight[kind], rows[...], row_by_col, preferred_element_type=f32
                 )
-                found = found + bias_ref[kind * local : (kind + 1) * local, :]
+                found = found + bias_ref[:, kind : kind + 1]
                 if kind == 2:
                     out[kind] = found.astype(bf16)
                     continue
@@ -730,7 +791,7 @@
         stage_keep = pltpu.make_async_copy(stage, both.at[here], single.at[7])
         stage_keep.start()
         near_step(2)
-        line_step(1, 1)
+        lines[1].step(1)
         turn_step(1)
         core_step(1)
         wide = hidden // 2
@@ -744,28 +805,30 @@
                 [up_bias_ref.at[:, span]],
             )
             if number == 0 and depth > 2:
-                line_step(1, 2)
+                lines[1].step(2)
         turn_step(3)
         core_step(3)
         turn_step(2)
         core_step(2)
         for k in range(3, depth):
-            line_step(1, k)
-        line_keep(1).wait()
+            lines[1].step(k)
+        lines[1].keep.wait()
         stage_keep.wait()
         arrive(both.at[there], single.at[5])
-        arrive(numbers_out, single.at[2])
-        for copy, condition in pending:
-            if condition is None:
-                copy.wait_send()
-            else:
-                pl.when(condition)(copy.wait_send)
+        for number in range(len(numbers)):
+            arrive(numbers_out[number], number_sems.at[1, number])
+        late_keep.wait()
+        for copy in pending:
+            copy.wait_send()
+        for run in lines:
+            run.end()
 
     out_shape = [
-        jax.ShapeDtypeStruct((vectors.shape[0], groups * shard), f32),
-        jax.ShapeDtypeStruct(numbers.shape, numbers.dtype),
+        jax.ShapeDtypeStruct((8, groups * shard), f32),
+        *[jax.ShapeDtypeStruct(v.shape, v.dtype) for v in numbers],
         jax.ShapeDtypeStruct((length, model), bf16),
         jax.ShapeDtypeStruct((length, early_width), bf16),
+        jax.ShapeDtypeStruct((own_len, model - early_width), bf16),
     ]
     out_shape += [
         jax.ShapeDtypeStruct(v.shape[:-2] + (groups * v.shape[-2], v.shape[-1]), v.dtype)
@@ -780,14 +843,20 @@
     results = pl.pallas_call(
         kernel,
         out_shape=tuple(out_shape),
-        in_specs=[VMEM] * (4 + weight_count) + [VMEM, ANY, ANY, ANY],
-        out_specs=(VMEM, VMEM) + (ANY,) * (len(out_shape) - 2),
+        in_specs=[VMEM] * (4 + len(vectors) + len(numbers) + weight_count),
+        out_specs=(VMEM,) * (1 + len(numbers)) + (ANY,) * (len(out_shape) - 1 - len(numbers)),
         scratch_shapes=[
-            pltpu.VMEM((groups,) + vectors.shape, f32),
+            pltpu.VMEM((groups, 8, shard), f32),
             pltpu.VMEM((own_len, model), bf16),
             pltpu.VMEM((kinds, count, length), bf16),
+            pltpu.VMEM((8, shard), f32),
+            pltpu.VMEM((local, kinds), f32),
+            pltpu.VMEM((1, hidden), f32),
+            pltpu.VMEM((half_rot, length), f32),
+            pltpu.VMEM((half_rot, length), f32),
             DMA((groups - 1,)),
             DMA((groups - 1,)),
+            DMA((2, len(numbers))),
             DMA((9,)),
             DMA((2, 2, depth - 1)),
             DMA((2, 2, depth - 1)),
@@ -804,127 +873,143 @@
         ),
         cost_estimate=pl.CostEstimate(flops=0, bytes_accessed=480_000_000, transcendentals=0),
         name="front",
-    )(tokens, cotangent, vectors, numbers, *weights, projection_bias, up_bias, cosine, sine)
+    )(tokens, cotangent, *vectors, *numbers, *weights, projection_bias, up_bias)
     return results[:-1]
 
 
-def exchange_attended(sizes, attended, activation, down_full, dense_full):
+class Held:
+    def __init__(self, sources, buffers, sems):
+        self.copies = {}
+        self.buffers = buffers
+        for number, (source, buffer) in enumerate(zip(sources, buffers)):
+            copy = pltpu.make_async_copy(source, buffer, sems.at[number])
+            copy.start()
+            self.copies[number] = copy
+
+    def __getitem__(self, number):
+        if number in self.copies:
+            self.copies.pop(number).wait()
+        return self.buffers[number]
+
+
+def buffers_for(*arrays):
+    return [pltpu.VMEM(v.shape, v.dtype) for v in arrays]
+
+
+def exchange_middle(
+    sizes, attended, activation, down_full, dense_full, cotangent_early, cotangent_late, slope
+):
     width, total = attended.shape
     length = total // 2
     rows, model = activation.shape[0], down_full.shape[0]
-
-    def kernel(attended_ref, activation_ref, down_ref, dense_ref, *rest):
-        full, block_out, feed, stage, sems = rest
+    hidden = slope.shape[1]
+    depth = sizes["tp"]
+    late_width = cotangent_late.shape[1]
+    holds = [activation, down_full, dense_full, cotangent_early, slope]
+
+    def kernel(attended_ref, cotangent_ref, *refs):
+        held_refs, refs = refs[: len(holds)], refs[len(holds) :]
+        full_out, block_out, late_out, both, grad_hidden, hidden_sum = refs[:6]
+        full, feed, late, made, *buffers, sems, held_sems, line_send, line_recv = refs[6:]
         place = Place(sizes)
-        greet([place.across()])
         here, there = place.half, 1 - place.half
 
         def tokens(half):
             return attended_ref.at[:, pl.ds(pl.multiple_of(half * length, length), length)]
 
-        away = send(
-            tokens(there), half_rows(full, here, width), sems.at[0], sems.at[1], place.across()
-        )
-        load = pltpu.make_async_copy(tokens(here), stage, sems.at[2])
-        keep = pltpu.make_async_copy(stage, half_rows(full, here, width), sems.at[3])
+        mine = half_rows(full, here, width)
+        load = pltpu.make_async_copy(tokens(here), mine, sems.at[0])
+        load.start()
+        held = Held(held_refs, buffers, held_sems)
+        greet_line(place, [place.across()])
+        line = Line(place, cotangent_ref, late, line_send, line_recv, sems.at[1])
+        line.start()
+        away = send(tokens(there), mine, sems.at[2], sems.at[3], place.across())
         away.start()
-        load.start()
+        half = model // 2
+        for number in range(2):
+            part = pl.ds(number * half, half)
+            multiply("nt", [(held[0], held[1].at[part])], [feed.at[:, part]])
+            if depth > number + 1:
+                line.step(number + 1)
         load.wait()
-        keep.start()
-        multiply("nt", [(activation_ref, down_ref)], [feed])
-        keep.wait()
         away.wait_send()
         came = half_rows(full, there, width)
-        send(came, came, sems.at[0], sems.at[1], place.across()).wait_recv()
+        send(came, came, sems.at[2], sems.at[3], place.across()).wait_recv()
+        full_keep = pltpu.make_async_copy(full, full_out, sems.at[4])
+        full_keep.start()
         multiply(
             "tt",
-            [(full, dense_ref)],
+            [(full, held[2])],
             [block_out],
             lambda found, before: (found + before,),
             [feed],
         )
+        for k in range(3, depth):
+            line.step(k)
+        line.keep.wait()
+        late_keep = pltpu.make_async_copy(late, late_out, sems.at[5])
+        late_keep.start()
+
+        def parts(weight):
+            first = model - late_width
+            return [
+                (held[3], weight.at[pl.ds(0, first)]),
+                (late, weight.at[pl.ds(first, late_width)]),
+            ]
+
+        multiply("tt", [(b, a) for a, b in parts(held[2])], [made])
+        away = send(
+            half_rows(made, there, width), both.at[here], sems.at[6], sems.at[7], place.across()
+        )
+        keep = pltpu.make_async_copy(half_rows(made, here, width), both.at[here], sems.at[8])
+        away.start()
+        keep.start()
+
+        def scaled(found, slope):
+            found = found * slope.astype(f32)
+            return found, jnp.sum(found, axis=0, keepdims=True)
+
+        multiply("nn", parts(held[1]), [grad_hidden, hidden_sum], scaled, [held[4]])
+        for copy in (keep, full_keep, late_keep):
+            copy.wait()
+        away.wait_send()
+        came = both.at[there]
+        send(came, came, sems.at[6], sems.at[7], place.across()).wait_recv()
+        line.end()
 
     return pl.pallas_call(
         kernel,
         out_shape=(
             jax.ShapeDtypeStruct((2 * width, length), bf16),
             jax.ShapeDtypeStruct((rows, model), bf16),
-            jax.ShapeDtypeStruct((rows, model), f32),
+            jax.ShapeDtypeStruct((rows, late_width), bf16),
+            jax.ShapeDtypeStruct((2, width, length), bf16),
+            jax.ShapeDtypeStruct((rows, hidden), bf16),
+            jax.ShapeDtypeStruct((1, hidden), f32),
         ),
-        in_specs=[ANY] * 4,
-        out_specs=(ANY,) * 3,
-        scratch_shapes=[pltpu.VMEM((width, length), bf16), DMA((4,))],
+        in_specs=[ANY] * (2 + len(holds)),
+        out_specs=(ANY,) * 5 + (VMEM,),
+        scratch_shapes=[
+            pltpu.VMEM((2 * width, length), bf16),
+            pltpu.VMEM((rows, model), f32),
+            pltpu.VMEM((rows, late_width), bf16),
+            pltpu.VMEM((2 * width, length), bf16),
+            *buffers_for(*holds),
+            DMA((9,)),
+            DMA((len(holds),)),
+            DMA((2, depth - 1)),
+            DMA((2, depth - 1)),
+        ],
         compiler_params=pltpu.CompilerParams(
             collective_id=4, has_side_effects=True, vmem_limit_bytes=60 << 20
         ),
-        cost_estimate=pl.CostEstimate(flops=0, bytes_accessed=90_000_000, transcendentals=0),
-        name="exchange_attended",
-    )(attended, activation, down_full, dense_full)[:2]
-
-
-def exchange_gradient(sizes, cotangents, dense_full, down_full, slope):
-    rows, hidden = slope.shape
-    local = dense_full.shape[1]
-    width = local // 2
-    count = len(cotangents)
-
-    def kernel(*refs):
-        cotangent_refs, (dense_ref, down_ref, slope_ref) = refs[:count], refs[count : count + 3]
-        both, grad_hidden, made, stage, sems = refs[count + 3 :]
-        place = Place(sizes)
-        greet([place.across()])
-        here, there = place.half, 1 - place.half
-
-        def parts(weight_ref):
-            found, first = [], 0
-            for ref in cotangent_refs:
-                found.append((ref, weight_ref.at[pl.ds(first, ref.shape[1])]))
-                first += ref.shape[1]
-            return found
-
-        multiply("tt", [(b, a) for a, b in parts(dense_ref)], [made])
-        away = send(
-            half_rows(made, there, width), both.at[here], sems.at[0], sems.at[1], place.across()
-        )
-        load = pltpu.make_async_copy(half_rows(made, here, width), stage, sems.at[2])
-        keep = pltpu.make_async_copy(stage, both.at[here], sems.at[3])
-        away.start()
-        load.start()
-        load.wait()
-        keep.start()
-        multiply(
-            "nn",
-            parts(down_ref),
-            [grad_hidden],
-            lambda found, slope: (found * slope.astype(f32),),
-            [slope_ref],
-        )
-        keep.wait()
-        away.wait_send()
-        came = both.at[there]
-        send(came, came, sems.at[0], sems.at[1], place.across()).wait_recv()
-
-    return pl.pallas_call(
-        kernel,
-        out_shape=(
-            jax.ShapeDtypeStruct((2, width, rows), bf16),
-            jax.ShapeDtypeStruct((rows, hidden), bf16),
-            jax.ShapeDtypeStruct((local, rows), bf16),
-        ),
-        in_specs=[ANY] * (count + 3),
-        out_specs=(ANY,) * 3,
-        scratch_shapes=[pltpu.VMEM((width, rows), bf16), DMA((4,))],
-        compiler_params=pltpu.CompilerParams(
-            collective_id=5, has_side_effects=True, vmem_limit_bytes=60 << 20
-        ),
-        cost_estimate=pl.CostEstimate(flops=0, bytes_accessed=85_000_000, transcendentals=0),
-        name="exchange_gradient",
-    )(*cotangents, dense_full, down_full, slope)[:2]
-
-
-def exchange_back(
-    sizes, back, normed, grad_hidden, cotangents, activation, up_full, projection
-):
+        cost_estimate=pl.CostEstimate(flops=0, bytes_accessed=140_000_000, transcendentals=0),
+        name="exchange_middle",
+    )(attended, cotangent_late, *holds)
+
+
+def exchange_back(sizes, back, normed, grad_hidden, cotangents, activation, up_full, projection):
     kinds, width, total = back.shape
     length = total // 2
     chips, halves = sizes["fsdp"] // 2, sizes["ctx"]
@@ -932,18 +1017,25 @@
     hidden = grad_hidden.shape[1]
     span = model // (2 * chips)
     shard = span // halves
-    side = shard // 2
-
+    sides = (shard // 4, shard // 2)
     count = len(cotangents)
 
-    def kernel(back_ref, normed_ref, hidden_ref, *rest):
-        cotangent_refs, rest = rest[:count], rest[count:]
-        (activation_ref, up_ref, weight_ref), rest = rest[:3], rest[3:]
-        full, sums, turns, block_in = rest[0], rest[1:3], rest[3:7], rest[7]
-        made_in, came_in, feed = rest[8:10], rest[10:12], rest[12]
-        stage, sems, core_send, core_recv, turn_send, turn_recv = rest[13:]
+    def kernel(back_ref, *rest):
+        held_refs, rest = rest[: 4 + count], rest[4 + count :]
+        weight_ref, full_out, made, came, turns, block_in, feed = (
+            rest[0],
+            rest[1],
+            rest[2:4],
+            rest[4:6],
+            rest[6:10],
+            rest[10],
+            rest[11],
+        )
+        full, diagonal, stage = rest[12:15]
+        buffers = rest[15 : 19 + count]
+        held_sems, sems, stage_sems, core_send, core_recv, turn_send, turn_recv = rest[19 + count :]
+        held = Held(held_refs, buffers, held_sems)
         place = Place(sizes)
-        greet(plane(place))
         here, there = place.half, 1 - place.half
         other = 1 - place.core
 
@@ -953,22 +1045,19 @@
         def heads(half):
             return full.at[:, pl.ds(pl.multiple_of(half * width, width), width)]
 
+        load = pltpu.make_async_copy(tokens(here), heads(here), sems.at[2])
+        load.start()
+        greet(plane(place))
         away = send(tokens(there), heads(here), sems.at[0], sems.at[1], place.across())
-        load = pltpu.make_async_copy(tokens(here), stage, sems.at[2])
-        keep = pltpu.make_async_copy(stage, heads(here), sems.at[3])
         away.start()
-        load.start()
-        load.wait()
-        keep.start()
 
         def to_pair(number):
-            made, came = made_in[number], came_in[number]
             copies = []
             for chip in range(chips):
                 copies.append(
                     send(
-                        made.at[pl.ds(pl.multiple_of((2 * chip + other) * span, 16), span)],
-                        came.at[pl.ds(chip * span, span)],
+                        made[number].at[pl.ds(pl.multiple_of((2 * chip + other) * span, 16), span)],
+                        came[number].at[pl.ds(chip * span, span)],
                         core_send.at[number, chip],
                         core_recv.at[number, chip],
                         place.pair(),
@@ -977,72 +1066,81 @@
                 copies[-1].start()
             return copies
 
-        def add_pair(number, copies):
-            made, came, out = made_in[number], came_in[number], sums[number]
+        def turn(number, copies):
             for copy in copies:
                 copy.wait()
-
-            def step(mine, theirs, out_ref):
-                out_ref[...] = (mine[...].astype(f32) + theirs[...].astype(f32)).astype(bf16)
-
-            wide = hidden // 2
-            pltpu.emit_pipeline(
-                step,
-                grid=(chips, 2),
-                in_specs=[
-                    pl.BlockSpec((span, wide), lambda i, j: (2 * i + place.core, j)),
-                    pl.BlockSpec((span, wide), lambda i, j: (i, j)),
-                ],
-                out_specs=[pl.BlockSpec((span, wide), lambda i, j: (i, j))],
-            )(made, came, out)
-
-        def turn(number):
-            out = sums[number]
-            copies = []
+            sent = []
             for k in range(1, chips):
-                block = (place.ahead(k) * halves + there) * shard
-                for way, device in enumerate(
-                    (place.across(), place.device(chip=place.ahead(k)))
-                ):
-                    copies.append(
+                chip = place.ahead(k)
+                mine = (place.block(chip, place.core, there)) * shard
+                theirs = (chip * halves + there) * shard
+                loads = (
+                    pltpu.make_async_copy(
+                        made[number].at[pl.ds(pl.multiple_of(mine, 16), shard)],
+                        stage.at[0],
+                        stage_sems.at[0],
+                    ),
+                    pltpu.make_async_copy(
+                        came[number].at[pl.ds(pl.multiple_of(theirs, 16), shard)],
+                        stage.at[1],
+                        stage_sems.at[1],
+                    ),
+                )
+                for copy in loads:
+                    copy.start()
+                for copy in loads:
+                    copy.wait()
+
+                @pl.loop(0, shard, step=16)
+                def _(r):
+                    at = pl.ds(pl.multiple_of(r, 16), 16)
+                    diagonal[number, k - 1, at, :] = (
+                        stage[0, at, :].astype(f32) + stage[1, at, :].astype(f32)
+                    ).astype(bf16)
+
+                for way, device in enumerate((place.across(), place.device(chip=chip))):
+                    side = sides[number]
+                    part = pl.ds(0, side) if way == 0 else pl.ds(side, shard - side)
+                    sent.append(
                         send(
-                            out.at[pl.ds(pl.multiple_of(block + way * side, 16), side)],
+                            diagonal.at[number, k - 1, part],
                             turns[2 * number + way].at[k - 1],
                             turn_send.at[number, way, k],
                             turn_recv.at[number, way, k],
                             device,
                         )
                     )
-                    copies[-1].start()
-            return copies
-
-        multiply("tn", [(normed_ref, hidden_ref)], [made_in[0]])
+                    sent[-1].start()
+            return sent
+
+        multiply("tn", [(held[0], held[1])], [made[0]])
         up_copies = to_pair(0)
         first = 0
-        for ref in cotangent_refs:
-            span_of = pl.ds(first, ref.shape[1])
-            multiply("tn", [(ref, activation_ref)], [made_in[1].at[span_of]])
+        for number in range(count):
+            ref = held[2 + number]
+            part = pl.ds(first, ref.shape[1])
+            multiply("tn", [(ref, held[2 + count])], [made[1].at[part]])
             first += ref.shape[1]
+            if number == 0:
+                turned = turn(0, up_copies)
         down_copies = to_pair(1)
-        add_pair(0, up_copies)
-        turned = turn(0)
-        multiply("nt", [(hidden_ref, up_ref)], [feed])
-        add_pair(1, down_copies)
-        turned += turn(1)
-        keep.wait()
+        half = model // 2
+        for number in range(2):
+            part = pl.ds(number * half, half)
+            multiply("nt", [(held[1], held[3 + count].at[part])], [feed.at[:, part]])
+            if number == 0:
+                turned += turn(1, down_copies)
+        load.wait()
         away.wait_send()
         send(heads(there), heads(there), sems.at[0], sems.at[1], place.across()).wait_recv()
-        flat = full.reshape(2 * kinds * width, length)
-
-        def step(left_ref, right_ref, before_ref, out_ref):
+        keep = pltpu.make_async_copy(full, full_out, sems.at[3])
+        keep.start()
+
+        def step(right_ref, before_ref, out_ref):
             found = before_ref[...]
             for kind in range(kinds):
-                rows_of = pl.ds(kind * 2 * width, 2 * width)
                 found += lax.dot_general(
-                    left_ref[rows_of, :],
-                    right_ref[kind],
-                    row_by_col,
-                    preferred_element_type=f32,
+                    full[kind], right_ref[kind], row_by_col, preferred_element_type=f32
                 )
             out_ref[...] = found.astype(bf16)
 
@@ -1051,108 +1149,210 @@
             step,
             grid=(model // tile,),
             in_specs=[
-                pl.BlockSpec(flat.shape, lambda n: (0, 0)),
                 pl.BlockSpec((kinds, tile, 2 * width), lambda n: (0, n, 0)),
                 pl.BlockSpec((rows, tile), lambda n: (0, n)),
             ],
             out_specs=[pl.BlockSpec((rows, tile), lambda n: (0, n))],
-        )(flat, weight_ref, feed, block_in)
+        )(weight_ref, feed, block_in)
+        keep.wait()
         for copy in turned:
             copy.wait()
 
     product = jax.ShapeDtypeStruct((model, hidden), bf16)
     part = jax.ShapeDtypeStruct((model // 2, hidden), bf16)
+    holds = [normed, grad_hidden, *cotangents, activation, up_full]
     results = pl.pallas_call(
         kernel,
         out_shape=(
             jax.ShapeDtypeStruct((kinds, 2 * width, length), bf16),
-            part,
-            part,
-            *[jax.ShapeDtypeStruct((chips - 1, side, hidden), bf16)] * 4,
-            jax.ShapeDtypeStruct((rows, model), bf16),
             product,
             product,
             part,
             part,
+            *[
+                jax.ShapeDtypeStruct((chips - 1, n, hidden), bf16)
+                for side in sides
+                for n in (side, shard - side)
+            ],
+            jax.ShapeDtypeStruct((rows, model), bf16),
             jax.ShapeDtypeStruct((rows, model), f32),
         ),
-        in_specs=[ANY] * (6 + count),
-        out_specs=(ANY,) * 13,
+        in_specs=[ANY] * (len(holds) + 2),
+        out_specs=(ANY,) * 11,
         scratch_shapes=[
-            pltpu.VMEM((kinds, width, length), bf16),
+            pltpu.VMEM((kinds, 2 * width, length), bf16),
+            pltpu.VMEM((2, chips - 1, shard, hidden), bf16),
+            pltpu.VMEM((2, shard, hidden), bf16),
+            *buffers_for(*holds),
+            DMA((len(holds),)),
             DMA((4,)),
+            DMA((2,)),
             DMA((2, chips)),
             DMA((2, chips)),
             DMA((2, 2, chips)),
             DMA((2, 2, chips)),
         ],
         compiler_params=pltpu.CompilerParams(
-            collective_id=6, has_side_effects=True, vmem_limit_bytes=60 << 20
+            collective_id=5, has_side_effects=True, vmem_limit_bytes=60 << 20
         ),
-        cost_estimate=pl.CostEstimate(flops=0, bytes_accessed=220_000_000, transcendentals=0),
+        cost_estimate=pl.CostEstimate(flops=0, bytes_accessed=180_000_000, transcendentals=0),
         name="exchange_back",
-    )(back, normed, grad_hidden, *cotangents, activation, up_full, projection)
-    return results[:8]
-
-
-def small_reduce(sizes, blocks):
-    count, depth = sizes["fsdp"] * sizes["ctx"], sizes["tp"]
-
-    def kernel(blocks_ref, out_ref, landed, line, send_sem, recv_sem, line_send, line_recv):
+    )(back, *holds, projection)
+    full, up_made, down_made, up_came, down_came, *turned = results[:9]
+    return full, [(up_made, up_came), (down_made, down_came)], turned, results[9]
+
+
+def finish_all(sizes, grad, tokens, cotangent, vectors, partials, splits):
+    chips, halves, depth = sizes["fsdp"] // 2, sizes["ctx"], sizes["tp"]
+    groups = sizes["fsdp"] * halves
+    own_len, model = tokens.shape
+    shard = model // groups
+    count = len(partials)
+    step_rows = 64
+
+    def kernel(grad_ref, tokens_ref, cotangent_ref, vector_ref, *refs):
+        partial_in, refs = refs[:count], refs[count:]
+        input_ref, small_ref = refs[:2]
+        weight_out, refs = refs[2 : 2 + count], refs[2 + count :]
+        near, refs = refs[:count], refs[count:]
+        sums, blocks, landed, line, near_send, near_recv, load_sem, *sems = refs
+        block_send, block_recv, line_send, line_recv = sems
         place = Place(sizes)
         peers = place.group()
         layers = [(place.layer + k) % depth for k in range(1, depth)]
         devices = [place.device(chip=a, core=b, half=c) for a, b, c in peers]
         greet(devices + [place.device(layer=k) for k in layers])
+        pending = []
+        for a in range(count):
+            targets = [place.across()] + [
+                place.device(chip=place.ahead(k)) for k in range(1, chips)
+            ]
+            for at, device in enumerate(targets):
+                pending.append(
+                    send(
+                        partial_in[a].at[at],
+                        near[a].at[at],
+                        near_send.at[a, at],
+                        near_recv.at[a, at],
+                        device,
+                    )
+                )
+                pending[-1].start()
+            pltpu.make_async_copy(
+                partial_in[a].at[chips], near[a].at[chips], load_sem.at[a]
+            ).start()
+
+        gain = vector_ref[0:1, :]
+        sums[...] = jnp.zeros_like(sums)
+
+        @pl.loop(0, own_len, step=step_rows)
+        def _(r):
+            at = pl.ds(pl.multiple_of(r, step_rows), step_rows)
+            values = tokens_ref[at, :].astype(f32)
+            centered = values - jnp.mean(values, axis=-1, keepdims=True)
+            spread = jnp.mean(centered * centered, axis=-1, keepdims=True)
+            scale = lax.rsqrt(spread + epsilon)
+            normal = centered * scale
+            found = grad_ref[at, :].astype(f32)
+            away = cotangent_ref[at, :].astype(f32)
+            inner = found * gain
+            mean = jnp.mean(inner, axis=-1, keepdims=True)
+            along = jnp.mean(inner * normal, axis=-1, keepdims=True)
+            input_ref[at, :] = (scale * (inner - mean - normal * along)).astype(bf16)
+            sums[0:1, :] += jnp.sum(found * normal, axis=0, keepdims=True)
+            sums[1:2, :] += jnp.sum(found, axis=0, keepdims=True)
+            sums[2:3, :] += jnp.sum(away, axis=0, keepdims=True)
+
+        for number in range(groups):
+            blocks[number] = sums[:, number * shard : (number + 1) * shard]
         copies = []
         for at, (chip, core, half) in enumerate(peers):
-            copy = send(
-                blocks_ref.at[place.block(chip, core, half)],
-                landed.at[at],
-                send_sem.at[at],
-                recv_sem.at[at],
-                devices[at],
+            copies.append(
+                send(
+                    blocks.at[place.block(chip, core, half)],
+                    landed.at[at],
+                    block_send.at[at],
+                    block_recv.at[at],
+                    devices[at],
+                )
             )
-            copy.start()
-            copies.append(copy)
-        total = blocks_ref[place.block()]
+            copies[-1].start()
+        total = blocks[place.block()]
         for at, copy in enumerate(copies):
             copy.wait()
             total += landed[at]
         line[0] = total
         copies = []
         for k, layer in enumerate(layers):
-            copy = send(
-                line.at[0],
-                line.at[k + 1],
-                line_send.at[k],
-                line_recv.at[k],
-                place.device(layer=layer),
+            copies.append(
+                send(
+                    line.at[0],
+                    line.at[k + 1],
+                    line_send.at[k],
+                    line_recv.at[k],
+                    place.device(layer=layer),
+                )
             )
-            copy.start()
-            copies.append(copy)
+            copies[-1].start()
         for k, copy in enumerate(copies):
             copy.wait()
             total += line[k + 1]
-        out_ref[...] = total
-
-    block = blocks.shape[1:]
+        small_ref[...] = total
+
+        for copy in pending:
+            copy.wait()
+        for a in range(count):
+            own = near[a].at[chips]
+            pltpu.make_async_copy(own, own, load_sem.at[a]).wait()
+            rows, width = partials[a].shape[1:]
+
+            @pl.loop(0, rows, step=16)
+            def _(r, a=a, width=width):
+                at = pl.ds(pl.multiple_of(r, 16), 16)
+                found = near[a][0, at, :].astype(f32)
+                for number in range(1, chips + 1):
+                    found += near[a][number, at, :].astype(f32)
+                if splits[a] == 1:
+                    weight_out[a][at, :] = found
+                else:
+                    wide = width // splits[a]
+                    for kind in range(splits[a]):
+                        weight_out[a][kind, at, :] = found[:, kind * wide : (kind + 1) * wide]
+
+    out_shape = [
+        jax.ShapeDtypeStruct((own_len, model), bf16),
+        jax.ShapeDtypeStruct((8, shard), f32),
+    ]
+    for v, n in zip(partials, splits):
+        rows, width = v.shape[1:]
+        out_shape.append(
+            jax.ShapeDtypeStruct((rows, width) if n == 1 else (n, rows, width // n), f32)
+        )
     return pl.pallas_call(
         kernel,
-        out_shape=jax.ShapeDtypeStruct(block, f32),
-        in_specs=[VMEM],
-        out_specs=VMEM,
+        out_shape=tuple(out_shape),
+        in_specs=[VMEM] * 4 + [ANY] * count,
+        out_specs=(VMEM,) * len(out_shape),
         scratch_shapes=[
-            pltpu.VMEM((count - 1,) + block, f32),
-            pltpu.VMEM((depth,) + block, f32),
-            DMA((count - 1,)),
-            DMA((count - 1,)),
+            *buffers_for(*partials),
+            pltpu.VMEM((8, model), f32),
+            pltpu.VMEM((groups, 8, shard), f32),
+            pltpu.VMEM((groups - 1, 8, shard), f32),
+            pltpu.VMEM((depth, 8, shard), f32),
+            DMA((count, chips)),
+            DMA((count, chips)),
+            DMA((count,)),
+            DMA((groups - 1,)),
+            DMA((groups - 1,)),
             DMA((depth - 1,)),
             DMA((depth - 1,)),
         ],
-        compiler_params=pltpu.CompilerParams(collective_id=3, has_side_effects=True),
-        name="small_reduce",
-    )(blocks)
+        compiler_params=pltpu.CompilerParams(
+            collective_id=3, has_side_effects=True, vmem_limit_bytes=60 << 20
+        ),
+        cost_estimate=pl.CostEstimate(flops=0, bytes_accessed=90_000_000, transcendentals=0),
+        name="finish_all",
+    )(grad, tokens, cotangent, vectors, *partials)
 
 
 def tile_at(number):
@@ -1443,22 +1643,14 @@
     half = lax.axis_index("ctx")
     total_len = 2 * half_len
 
-    vectors = jnp.concatenate([norm_gain, norm_bias, dense_bias, down_bias]).astype(f32)
-    vectors = jnp.pad(vectors.reshape(4, shard_rows), ((0, 4), (0, 0)))
-    numbers = jnp.pad(jnp.concatenate([segments, positions], axis=0), ((0, 6), (0, 0)))
-    exponent = jnp.arange(ROT // 2, dtype=f32) * 2.0 / ROT
-    inverse = 10000.0 ** (-exponent)
-
-    def angles(places_of):
-        phase_angle = inverse[:, None] * places_of.astype(f32)[None, :]
-        return jnp.cos(phase_angle), jnp.sin(phase_angle)
-
-    cosine_own, sine_own = angles(positions[0])
+    numbers = [segments, positions]
     (
         vectors_full,
-        numbers_other,
+        segments_other,
+        positions_other,
         normed,
         cotangent_early,
+        cotangent_late,
         projection,
         up_full,
         dense_full,
@@ -1470,19 +1662,12 @@
         sizes,
         tokens[0],
         cotangent[0],
-        vectors,
+        [norm_gain, norm_bias, dense_bias, down_bias],
         numbers,
         [projection_weight.transpose(1, 0, 2), up_weight, dense_weight, down_weight],
-        projection_bias.astype(f32).reshape(3 * local_width, 1),
-        up_bias.astype(f32)[None, :],
-        cosine_own,
-        sine_own,
+        projection_bias,
+        up_bias,
     )
-    gain_full, shift_full, bias_dense, bias_down = (vectors_full[row] for row in range(4))
-
-    cotangent_late, normed = ordered(cotangent[0, :, cotangent_early.shape[1] :], normed)
-    cotangent_late = lax.all_gather(cotangent_late, "tp", axis=0, tiled=True)
-    cotangents = [cotangent_early, cotangent_late]
 
     def in_order(own, other, axis):
         return jnp.where(
@@ -1491,8 +1676,8 @@
             jnp.concatenate([other, own], axis=axis),
         )
 
-    sequence = in_order(numbers, numbers_other, 1)
-    segment_row, position_row = sequence[0], sequence[1]
+    segment_row = in_order(segments[0], segments_other[0], 0)
+    position_row = in_order(positions[0], positions_other[0], 0)
     places = jnp.arange(total_len, dtype=jnp.int32)
     edges = jnp.concatenate([jnp.ones((1,), bool), segment_row[1:] != segment_row[:-1]])
     start = lax.cummax(jnp.where(edges, places, 0))
@@ -1502,15 +1687,22 @@
         jnp.maximum((start[TILE - 1 :: TILE] + TILE - 1) // TILE, low),
         jnp.arange(tile_count, dtype=jnp.int32),
     )
-    cosine_full, sine_full = angles(position_row)
+    exponent = jnp.arange(ROT // 2, dtype=f32) * 2.0 / ROT
+    phase_angle = (10000.0 ** (-exponent))[:, None] * position_row.astype(f32)[None, :]
+    cosine_full, sine_full = jnp.cos(phase_angle), jnp.sin(phase_angle)
     attended_heads, log_sum = attend(low, mid, both, start[None, :])
-    attended, block_out = exchange_attended(
-        sizes, attended_heads, activation, down_full, dense_full
+    attended, block_out, cotangent_late, grad_both, grad_hidden, hidden_sum = exchange_middle(
+        sizes,
+        attended_heads,
+        activation,
+        down_full,
+        dense_full,
+        cotangent_early,
+        cotangent_late,
+        slope,
     )
+    cotangents = [cotangent_early, cotangent_late]
     branch_own = lax.psum_scatter(block_out, "tp", scatter_dimension=0, tiled=True)
-    cotangent_late, block_out = ordered(cotangent_late, block_out)
-    cotangents = [cotangent_early, cotangent_late]
-    grad_both, grad_hidden = exchange_gradient(sizes, cotangents, dense_full, down_full, slope)
     back_heads = attend_back(
         low,
         mid,
@@ -1522,37 +1714,41 @@
         cosine_full,
         sine_full,
     )
-    grad_projected, up_sum, down_sum, *turned, block_in = exchange_back(
+    grad_projected, paired, turned, block_in = exchange_back(
         sizes, back_heads, normed, grad_hidden, cotangents, activation, up_full, projection
     )
     grad_projected = grad_projected.reshape(3 * local_width, half_len)
     block_in, branch_own = ordered(block_in, branch_own)
-    grad_normed_own = lax.psum_scatter(block_in, "tp", scatter_dimension=0, tiled=True).astype(f32)
-    hidden_sum = jnp.sum(grad_hidden.astype(f32), axis=0)
+    grad_normed_own = lax.psum_scatter(block_in, "tp", scatter_dimension=0, tiled=True)
     projected_sum = jnp.sum(grad_projected.astype(f32), axis=1)
-    small = jnp.concatenate([projected_sum, hidden_sum]).reshape(-1, 128)
-    groups = sizes["fsdp"] // 2 * sizes["ctx"]
-    up_part, down_part, projection_part, dense_part, small_total = reduce(
+    small = jnp.concatenate([projected_sum, hidden_sum[0]]).reshape(-1, 128)
+    *pieces, small_total, partial = reduce(
         sizes,
-        [v.reshape(groups, shard_rows, hidden_width) for v in (up_sum, down_sum)],
+        paired,
         turned,
-        [([normed], grad_projected), (cotangents, attended)],
-        [1, 1, 3, 1],
+        [(cotangents, attended), ([normed], grad_projected)],
         small,
         2,
         "reduce_weights",
     )
-    tokens_late, grad_normed_own = ordered(tokens[0], grad_normed_own)
-    inputs = tokens_late.astype(f32)
-    _, norm_pull = jax.vjp(layer_norm, inputs, gain_full, shift_full)
-    layer_output = (inputs + branch_own.astype(f32) + (bias_dense + bias_down)).astype(bf16)
-    cotangent_own = cotangent[0].astype(f32)
-    grad_inputs, grad_gain, grad_shift = norm_pull(grad_normed_own)
-    input_grad = grad_inputs + cotangent_own
-    output_sum = jnp.sum(cotangent_own, axis=0)
-    sums = jnp.stack([grad_gain, grad_shift, output_sum]).reshape(3, -1, shard_rows)
-    sums = jnp.pad(sums.transpose(1, 0, 2), ((0, 0), (0, 5), (0, 0)))
-    totals = small_reduce(sizes, sums)
+    up_part, down_part, dense_part = (jnp.sum(v.astype(f32), axis=0) for v in pieces)
+    up_part, down_part, dense_part, grad_normed_own = ordered(
+        up_part, down_part, dense_part, grad_normed_own
+    )
+    input_part, totals, projection_part = finish_all(
+        sizes,
+        grad_normed_own,
+        tokens[0],
+        cotangent[0],
+        vectors_full,
+        [partial],
+        [3],
+    )
+    bias_dense, bias_down = vectors_full[2], vectors_full[3]
+    layer_output = (
+        tokens[0].astype(f32) + branch_own.astype(f32) + (bias_dense + bias_down)
+    ).astype(bf16)
+    input_grad = cotangent[0].astype(f32) + input_part.astype(f32)
     small_flat = small_total.reshape(-1)
     return (
         layer_output[None],

time: 497 us -> 443 us (0.89); the launches traced: 494 us -> 435 us
  Pallas kernels: 426 us -> 390 us
  starting transfers between devices: 11.7 us -> 0.08 us
  local copies, waits for them, and re-layouts: 22.4 us -> 13.4 us
    pallas_call x1, Pallas kernels: 77.4 us -> 56.8 us  [exchange_back(): pl.pallas_call(kernel, out_shape=(jax.ShapeDtypeStruct((kinds, 2 * width,...]
    reduce_scatter x1, starting transfers between devices: 11.7 us -> 0.04 us  [body(): lax.psum_scatter(block_out, 'tp', scatter_dimension=0, tiled=True)]
    pallas_call x4 -> x3, Pallas kernels: 151 us -> 142 us  [the longest x1 73.2 us: reduce(): pl.pallas_call(kernel, out_shape=tuple(shapes + held_shapes + made_shapes...]
    unnamed x37 -> x32, local copies, waits for them, and re-layouts: 14.8 us -> 8.94 us
    pallas_call x1, Pallas kernels: 37.9 us -> 32.8 us  [attend_back(): pl.pallas_call(attend_back_kernel, out_shape=jax.ShapeDtypeStruct((3, wid...]
  transfers between devices with their start and end apart: 3 -> 2, of which waited for: 0 -> 0; matrix products, arithmetic and copies ran while one was open for 2% -> 3% of each run, Pallas kernels for 56% -> 37%
where the time goes in v1:
time: 443 us; the launch traced here: 435 us
  Pallas kernels  390 us (88%)
  other arithmetic  16.5 us (4%)
  between operations  14.7 us (3%)
  local copies, waits for them, and re-layouts  13.4 us (3%)
    pallas_call x1, Pallas kernels, front(): pl.pallas_call(kernel, out_shape=tuple(out_shape), in_specs=[VMEM] * (4 +...  141 us
    pallas_call x1, Pallas kernels, reduce(): pl.pallas_call(kernel, out_shape=tuple(shapes + held_shapes + made_shapes...  73.2 us
    pallas_call x1, Pallas kernels, exchange_back(): pl.pallas_call(kernel, out_shape=(jax.ShapeDtypeStruct((kinds, 2 * width,...  56.8 us
    pallas_call x1, Pallas kernels, exchange_middle(): pl.pallas_call(kernel, out_shape=(jax.ShapeDtypeStruct((2 * width, length...  39.9 us
    pallas_call x1, Pallas kernels, attend_back(): pl.pallas_call(attend_back_kernel, out_shape=jax.ShapeDtypeStruct((3, wid...  32.8 us
    pallas_call x1, Pallas kernels, finish_all(): pl.pallas_call(kernel, out_shape=tuple(out_shape), in_specs=[VMEM] * 4 +...  28.8 us
    pallas_call x1, Pallas kernels, attend(): pl.pallas_call(attend_kernel, out_shape=(jax.ShapeDtypeStruct((width, tot...  17 us
    unnamed x32, local copies, waits for them, and re-layouts  8.94 us
  transfers between devices with their start and end apart: 2, of which 0 were waited for; matrix products, arithmetic and copies ran while one was open for 3% of the time, Pallas kernels for 37%

profile of v1, /device:TPU:0, one launch (start us, length us, event | category | flops | bytes accessed | tf_op | source)
XLA Modules:
  0.0 434.6 jit_solution(15590077553245134696)
XLA Ops:
  7.3 141.5 %front.1 = (f32[8,2048]{1,0:T(8,128)}, s32[1,1024]{1,0:T(1,128)}, s32[1,1024]{1,0:T(1,128)}, bf16[1024,2048]{1,0:T(8,128)(2,1)}, bf16[1024,1536]{1,0:T(8,128)(2,...) custom-call(bf16[256,2048]{1,0:T(8,128)(2,1)} %bitcast.34, ...), custom_call_target="tpu_custom_call" | custom-call | bytes 480000000 | tf_op jit(solution)/shard_map/front/pallas_call | solution.py:843
  148.8 0.8 add_select_fusion
  149.7 0.3 reduce-window.9
  150.1 0.1 slice_reduce_fusion
  150.4 0.1 slice.50
  150.6 1.9 copy-done.3
  152.5 17.0 %attend.1 = (bf16[256,2048]{1,0:T(8,128)(2,1)S(1)}, f32[4,1,2048]{2,1,0:T(1,128)S(1)}) custom-call(s32[8]{0:T(128)S(1)} %get-tuple-element.103.low_ref, s32[8]{0:T(128)S(1)} %get-tuple-element.102.mid_ref, bf16[2,3,256,1024]{3,2,1,0:T(8,128)(2,1)S(1)} %copy-done.3, s32[1,2048]{1,0:T(1,128)S(1)} %bitcast.31), custom_call_target="tpu_custom_call" | custom-call | flops 17895692288 | bytes 4194304 | tf_op jit(solution)/shard_map/attend/pallas_call | solution.py:1565
  169.5 1.0 copy-done.1
  170.4 39.9 %exchange_middle.1 = (bf16[512,1024]{1,0:T(8,128)(2,1)}, bf16[1024,2048]{1,0:T(8,128)(2,1)}, bf16[1024,512]{1,0:T(8,128)(2,1)}, bf16[2,256,1024]{2,1,0:T(8,128)(...) custom-call(bf16[256,2048]{1,0:T(8,128)(2,1)} %copy-done.1, bf16[256,512]{1,0:T(8,128)(2,1)} %get-tuple-element.60.cotangent_ref, ...), custom_call_target="tpu_custom_call" | custom-call | bytes 140000000 | tf_op jit(solution)/shard_map/exchange_middle/pallas_call | solution.py:981
  210.4 0.5 multiply_sine_fusion
  211.0 0.6 copy-done.2
  211.5 0.3 copy-done.4
  211.9 32.8 %attend_back.1.back_ref = bf16[3,256,2048]{2,1,0:T(8,128)(2,1)S(1)} custom-call(s32[8]{0:T(128)S(1)} %get-tuple-element.103.low_ref, s32[8]{0:T(128)S(1)} %get-tuple-element.102.mid_ref, bf16[2,3,256,1024]{3,2,1,0:T(8,128)(2,1)} %get-tuple-element.58.triple_ref, bf16[2,256,1024]{2,1,0:T(8,128)(2,1)S(1)} %copy-done.4, bf16[256,2048]{1,0:T(8,128)(2,1)S(1)} %copy-done.2, ...), custom_call_target="tpu_custom_call" | custom-call | flops 35791384576 | bytes 6291456 | tf_op jit(solution)/shard_map/attend_back/pallas_call | solution.py:1587
  244.7 1.6 copy-done
  246.3 56.8 %exchange_back.1 = (bf16[3,512,1024]{2,1,0:T(8,128)(2,1)}, bf16[2048,2048]{1,0:T(8,128)(2,1)}, bf16[2048,2048]{1,0:T(8,128)(2,1)}, bf16[1024,2048]{1,0:T(8,128)(...) custom-call(bf16[3,256,2048]{2,1,0:T(8,128)(2,1)} %copy-done, ...), custom_call_target="tpu_custom_call" | custom-call | bytes 180000000 | tf_op jit(solution)/shard_map/exchange_back/pallas_call | solution.py:1164
  303.1 1.8 copy-done.5
  305.0 0.5 convert_reduce_fusion.2
  305.5 0.6 maximum_bitcast_fusion.refs_13_
  306.1 73.2 %reduce_weights.1 = (bf16[3,256,2048]{2,1,0:T(8,128)(2,1)}, bf16[3,256,2048]{2,1,0:T(8,128)(2,1)}, bf16[3,256,512]{2,1,0:T(8,128)(2,1)}, f32[28,128]{1,0:T(8,128...) custom-call(bf16[2048,2048]{1,0:T(8,128)(2,1)} %get-tuple-element.78.refs_0_, ...), custom_call_target="tpu_custom_call" | custom-call | bytes 400000000 | tf_op jit(solution)/shard_map/reduce_weights/pallas_call | solution.py:477
  379.3 0.7 slice.55
  380.0 0.6 reshape.113
  380.6 2.2 convert_reduce_fusion.3
  382.8 1.3 slice_bitcast_fusion
  384.1 4.0 convert_reduce_fusion.1
  388.2 2.0 convert_reduce_fusion
  390.2 0.9 slice_add_fusion
  391.1 1.4 fusion
  392.5 28.8 %finish_all.1 = (bf16[256,2048]{1,0:T(8,128)(2,1)}, f32[8,256]{1,0:T(8,128)}, f32[3,256,512]{2,1,0:T(8,128)}) custom-call(bf16[256,2048]{1,0:T(8,128)(2,1)} %reduce-scatter.5.cloned.1.call-done.grad_ref, bf16[256,2048]{1,0:T(8,128)(2,1)} %bitcast.35, bf16[256,2048]{1,0:T(8,128)(2,1)} %bitcast.37, f32[8,2048]{1,0:T(8,128)} %get-tuple-element.77.vector_ref, ...), custom_call_target="tpu_custom_call" | custom-call | bytes 90000000 | tf_op jit(solution)/shard_map/finish_all/pallas_call | solution.py:1331
  421.3 1.4 fusion.2
  422.7 2.9 add_bitcast_fusion
  425.6 0.6 copy.28
  426.2 1.1 copy.29
  (40 shorter events, 0.7 us)
Async XLA Ops:
  7.2 141.6 %copy-start.12 = (s32[1,1024]{1,0:T(1,128)S(1)}, s32[1,1024]{1,0:T(1,128)}, u32[]{:S(2)}) copy-start(s32[1,1024]{1,0:T(1,128)} %refs_7_.1) | copy-start | bytes 12292
  7.2 141.6 %copy-start.11 = (s32[1,1024]{1,0:T(1,128)S(1)}, s32[1,1024]{1,0:T(1,128)}, u32[]{:S(2)}) copy-start(s32[1,1024]{1,0:T(1,128)} %refs_6_.1) | copy-start | bytes 12292
  7.2 295.9 %reduce-scatter.3.cloned.1.call-start = ((), (), s32[]{:S(2)}) async-start(), calls=%async_computation.2 | async-start | bytes 5242880 | tf_op jit(solution)/shard_map/reduce_scatter | solution.py:1705
  150.6 1.9 copy-start.3
  169.5 1.0 copy-start.1
  210.3 1.2 copy-start.2
  210.3 1.5 copy-start.4
  210.4 182.1 %reduce-scatter.5.cloned.1.call-start = ((), (), s32[]{:S(2)}) async-start(), calls=%async_computation.3 | async-start | bytes 5242880 | tf_op jit(solution)/shard_map/reduce_scatter | solution.py:1722
  244.7 1.6 copy-start
  303.1 1.9 copy-start.5
  303.1 2.4 copy-start.13
  380.6 7.6 %copy-start.8 = (bf16[3,256,2048]{2,1,0:T(8,128)(2,1)S(1)}, bf16[3,256,2048]{2,1,0:T(8,128)(2,1)}, u32[]{:S(2)}) copy-start(bf16[3,256,2048]{2,1,0:T(8,128)(2,1)} %get-tuple-element.90) | copy-start | bytes 9437188
  388.2 2.9 copy-start.6
  388.2 2.9 copy-start.10
  392.5 30.3 %copy-start.7 = (bf16[1,256,2048]{2,1,0:T(8,128)(2,1)S(1)}, bf16[1,256,2048]{2,1,0:T(8,128)(2,1)}, u32[]{:S(2)}) copy-start(bf16[1,256,2048]{2,1,0:T(8,128)(2,1)} %param.27) | copy-start | bytes 3145732
  421.3 4.9 %copy-start.9 = (f32[3,256,512]{2,1,0:T(8,128)S(1)}, f32[3,256,512]{2,1,0:T(8,128)}, u32[]{:S(2)}) copy-start(f32[3,256,512]{2,1,0:T(8,128)} %get-tuple-element.97) | copy-start | bytes 4718596
  422.7 4.6 %copy-start.14 = (f32[1,256]{1,0:T(1,128)}, f32[1,256]{1,0:T(1,128)S(1)}, u32[]{:S(2)}) copy-start(f32[1,256]{1,0:T(1,128)S(1)} %get-tuple-element.106) | copy-start | bytes 3076
Sparse Core Ops, SparseCore 0:
  210.5 75.1 reduce-scatter.2
  303.3 75.2 reduce-scatter.4
